TPU v7x, 32 devices: a whole 2x2x4 slice. The times are simulated.
32 devices in a mesh: dp: 8 (over z, x), row: 2 (over y), col: 2 (over core).
Axes of the slice: x: 2, y: 2, z: 4, core: 2. Of those that a mesh axis runs over, the one named last changes fastest.
Arguments:
- inputs: bfloat16 [32768, 640], P('dp', ('row', 'col')), may hold values from -6 to 6
- cotangent: bfloat16 [32768, 640], P('dp', ('row', 'col')), may hold values from -6 to 6
- query_weight: bfloat16 [640, 1024], P('row', 'col'), may hold values from -0.25 to 0.25
- keyval_weight: bfloat16 [640, 512], P('row'), may hold values from -0.25 to 0.25
- out_weight: bfloat16 [1024, 640], P('col', 'row'), may hold values from -0.1875 to 0.1875
- gate_weight: bfloat16 [640, 2048], P('row', 'col'), may hold values from -0.25 to 0.25
- up_weight: bfloat16 [640, 2048], P('row', 'col'), may hold values from -0.25 to 0.25
- down_weight: bfloat16 [2048, 640], P('col', 'row'), may hold values from -0.125 to 0.125
- attend_in_gain: float32 [640], P(('row', 'col')), may hold values from -0.4 to 0.4
- attend_out_gain: float32 [640], P(('row', 'col')), may hold values from -0.4 to 0.4
- forward_in_gain: float32 [640], P(('row', 'col')), may hold values from -0.4 to 0.4
- forward_out_gain: float32 [640], P(('row', 'col')), may hold values from -0.4 to 0.4
- query_gain: float32 [256], replicated, may hold values from -0.4 to 0.4
- key_gain: float32 [256], replicated, may hold values from -0.4 to 0.4
Outputs:
- output: bfloat16 [32768, 640], P('dp', ('row', 'col'))
- input_grad: float32 [32768, 640], P('dp', ('row', 'col'))
- query_weight_grad: float32 [640, 1024], P('row', 'col')
- keyval_weight_grad: float32 [640, 512], P('row')
- out_weight_grad: float32 [1024, 640], P('col', 'row')
- gate_weight_grad: float32 [640, 2048], P('row', 'col')
- up_weight_grad: float32 [640, 2048], P('row', 'col')
- down_weight_grad: float32 [2048, 640], P('col', 'row')
- attend_in_gain_grad: float32 [640], P(('row', 'col'))
- attend_out_gain_grad: float32 [640], P(('row', 'col'))
- forward_in_gain_grad: float32 [640], P(('row', 'col'))
- forward_out_gain_grad: float32 [640], P(('row', 'col'))
- query_gain_grad: float32 [256], replicated
- key_gain_grad: float32 [256], replicated
All inputs are finite; a program needn't handle non-finite values.
Results may differ from a plain program's by a relative error of at most 0.018.
Values may be sent and summed in bfloat16 or wider, within the bound.
No kernel may reach another device: no remote copies, remote signals or barrier semaphores. Data moves between devices by JAX's collectives and lax.ppermute only.
A program may use at most 192 MiB of HBM per device.

v0:
```python
from functools import partial

import jax
import jax.numpy as jnp
from jax import lax
from jax.sharding import PartitionSpec as P

D = 640
HEAD_DIM = 256
WINDOW = 512
LEN = 4096


EPSILON = 1e-06
ROPE_BASE = 10000.0
MASKED = -1e30


def feature_stats(values):
    return lax.psum(values, ("row", "col"))


def gather_features(values):
    return lax.all_gather(values, "col", axis=1, tiled=True)


def partial_rows(values):
    return lax.psum_scatter(values, "row", scatter_dimension=1, tiled=True)


def gather_hidden(values):
    return lax.all_gather(values, "row", axis=1, tiled=True)


def partial_cols(values):
    return lax.psum_scatter(values, "col", scatter_dimension=1, tiled=True)


def rms_scale(values, offset):
    mean_sq = jnp.mean(values * values, axis=-1, keepdims=True)
    return values * lax.rsqrt(mean_sq + EPSILON) * (1.0 + offset)


def rotate(values, cosine, sine):
    half_dim = values.shape[-1] // 2
    first_half = values[..., :half_dim]
    second_half = values[..., half_dim:]
    return jnp.concatenate(
        [first_half * cosine - second_half * sine, second_half * cosine + first_half * sine],
        axis=-1,
    )


def rope_tables():
    half_dim = HEAD_DIM // 2
    frequency = ROPE_BASE ** (-(jnp.arange(half_dim, dtype=jnp.float32) * 2.0 / HEAD_DIM))
    angles = jnp.arange(LEN, dtype=jnp.float32)[:, None] * frequency[None, :]
    return (jnp.cos(angles), jnp.sin(angles))


def norm_forward(values, offset):
    row_total = feature_stats(jnp.sum(values * values, axis=-1, keepdims=True))
    scale_rows = lax.rsqrt(row_total / D + EPSILON)
    return (values * scale_rows * (1.0 + offset), scale_rows)


def norm_backward(values, scale_rows, offset, gradient):
    unit_rows = values * scale_rows
    scaled = gradient * (1.0 + offset)
    row_inner = feature_stats(jnp.sum(scaled * unit_rows, axis=-1, keepdims=True))
    return (
        scale_rows * (scaled - unit_rows * (row_inner / D)),
        jnp.sum(gradient * unit_rows, axis=0),
    )


def block_scores(query_block, key_window, first_row):
    block_rows = query_block.shape[1]
    key_span = key_window.shape[1]
    scores = jnp.einsum("sqd,skd->sqk", query_block, key_window, preferred_element_type=jnp.float32)
    query_pos = first_row + jnp.arange(block_rows, dtype=jnp.int32)[:, None]
    key_pos = first_row - WINDOW + jnp.arange(key_span, dtype=jnp.int32)[None, :]
    keep_mask = (query_pos - key_pos < WINDOW) & (query_pos >= key_pos) & (key_pos >= 0)
    return jnp.where(keep_mask[None], scores, MASKED)


def attend(query_rows, key_rows, value_rows):
    sequences = query_rows.shape[0]
    block_rows = min(512, LEN // 2)
    block_count = LEN // block_rows
    key_span = block_rows + WINDOW
    front_pad = ((0, 0), (WINDOW, 0), (0, 0))
    key_pad = jnp.pad(key_rows, front_pad)
    value_pad = jnp.pad(value_rows, front_pad)

    def one_block(first_row):
        query_block = lax.dynamic_slice_in_dim(query_rows, first_row, block_rows, 1)
        scores = block_scores(
            query_block, lax.dynamic_slice_in_dim(key_pad, first_row, key_span, 1), first_row
        )
        row_max = jnp.max(scores, axis=-1, keepdims=True)
        weights = jnp.exp(scores - row_max)
        row_total = jnp.sum(weights, axis=-1, keepdims=True)
        softmax_low = (weights / row_total).astype(jnp.bfloat16)
        value_window = lax.dynamic_slice_in_dim(value_pad, first_row, key_span, 1)
        result = jnp.einsum(
            "sqk,skd->sqd", softmax_low, value_window, preferred_element_type=jnp.float32
        )
        return (result, row_max + jnp.log(row_total))

    block_starts = jnp.arange(block_count, dtype=jnp.int32) * block_rows
    results, log_sums = lax.map(one_block, block_starts)
    attended = results.transpose(1, 0, 2, 3).reshape(sequences, LEN, HEAD_DIM)
    log_total = log_sums.transpose(1, 0, 2, 3).reshape(sequences, LEN, 1)
    return (attended, log_total)


def attend_back(query_rows, key_rows, value_rows, log_total, heads_grad):
    sequences = query_rows.shape[0]
    block_rows = min(512, LEN // 2)
    block_count = LEN // block_rows
    key_span = block_rows + WINDOW
    front_pad = ((0, 0), (WINDOW, 0), (0, 0))
    key_pad = jnp.pad(key_rows, front_pad)
    value_pad = jnp.pad(value_rows, front_pad)

    def one_block(accumulated, first_row):
        key_sum, value_sum = accumulated
        query_block = lax.dynamic_slice_in_dim(query_rows, first_row, block_rows, 1)
        grad_block = lax.dynamic_slice_in_dim(heads_grad, first_row, block_rows, 1)
        log_block = lax.dynamic_slice_in_dim(log_total, first_row, block_rows, 1)
        key_window = lax.dynamic_slice_in_dim(key_pad, first_row, key_span, 1)
        value_window = lax.dynamic_slice_in_dim(value_pad, first_row, key_span, 1)
        scores = block_scores(query_block, key_window, first_row)
        softmax_out = jnp.exp(scores - log_block)
        softmax_low = softmax_out.astype(jnp.bfloat16)
        softmax_grad = jnp.einsum(
            "sqd,skd->sqk", grad_block, value_window, preferred_element_type=jnp.float32
        )
        row_inner = jnp.sum(softmax_grad * softmax_out, axis=-1, keepdims=True)
        score_grad = (softmax_out * (softmax_grad - row_inner)).astype(jnp.bfloat16)
        query_part = jnp.einsum(
            "sqk,skd->sqd", score_grad, key_window, preferred_element_type=jnp.float32
        )
        key_part = jnp.einsum(
            "sqk,sqd->skd", score_grad, query_block, preferred_element_type=jnp.float32
        )
        value_part = jnp.einsum(
            "sqk,sqd->skd", softmax_low, grad_block, preferred_element_type=jnp.float32
        )
        key_old = lax.dynamic_slice_in_dim(key_sum, first_row, key_span, 1)
        value_old = lax.dynamic_slice_in_dim(value_sum, first_row, key_span, 1)
        key_sum = lax.dynamic_update_slice_in_dim(key_sum, key_old + key_part, first_row, 1)
        value_sum = lax.dynamic_update_slice_in_dim(value_sum, value_old + value_part, first_row, 1)
        return ((key_sum, value_sum), query_part)

    zero_sums = jnp.zeros((sequences, LEN + WINDOW, HEAD_DIM), jnp.float32)
    block_starts = jnp.arange(block_count, dtype=jnp.int32) * block_rows
    (key_sum, value_sum), query_parts = lax.scan(one_block, (zero_sums, zero_sums), block_starts)
    query_back = query_parts.transpose(1, 0, 2, 3).reshape(sequences, LEN, HEAD_DIM)
    return (query_back, key_sum[:, WINDOW:], value_sum[:, WINDOW:])


def per_device(
    inputs,
    cotangent,
    query_weight,
    keyval_weight,
    out_weight,
    gate_weight,
    up_weight,
    down_weight,
    attend_in_gain,
    attend_out_gain,
    forward_in_gain,
    forward_out_gain,
    query_gain,
    key_gain,
):
    tokens = inputs.shape[0]
    sequences = tokens // LEN
    residual = inputs.astype(jnp.float32)
    cosine, sine = rope_tables()
    attend_in, scale_in = norm_forward(residual, attend_in_gain)
    features_in = gather_features(attend_in.astype(jnp.bfloat16))
    query_raw = partial_rows(jnp.dot(features_in, query_weight, preferred_element_type=jnp.float32))
    keyval_raw = lax.psum(
        jnp.dot(features_in, keyval_weight, preferred_element_type=jnp.float32), "row"
    )
    key_raw = keyval_raw[:, :HEAD_DIM].reshape(sequences, LEN, HEAD_DIM)
    value_rows = keyval_raw[:, HEAD_DIM:].astype(jnp.bfloat16).reshape(sequences, LEN, HEAD_DIM)

    def query_prep(raw_rows, gain_rows):
        return rotate(rms_scale(raw_rows, gain_rows), cosine, sine) * HEAD_DIM ** (-0.5)

    def key_turn(normed_rows):
        return rotate(normed_rows, cosine, sine)

    query_shaped = query_raw.reshape(sequences, LEN, HEAD_DIM)
    query_ready, query_pullback = jax.vjp(query_prep, query_shaped, query_gain)
    query_rows = query_ready.astype(jnp.bfloat16)
    key_normed, key_norm_pullback = jax.vjp(rms_scale, key_raw, key_gain)
    key_ready, key_turn_pullback = jax.vjp(key_turn, key_normed)
    key_rows = key_ready.astype(jnp.bfloat16)
    attended, log_total = attend(query_rows, key_rows, value_rows)
    mixed_heads = attended.reshape(tokens, HEAD_DIM).astype(jnp.bfloat16)
    heads_wide = gather_hidden(mixed_heads)
    branch_attn = partial_cols(jnp.dot(heads_wide, out_weight, preferred_element_type=jnp.float32))
    attn_normed, scale_attn = norm_forward(branch_attn, attend_out_gain)
    hidden_state = residual + attn_normed
    forward_in, scale_mid = norm_forward(hidden_state, forward_in_gain)
    features_mid = gather_features(forward_in.astype(jnp.bfloat16))
    gate_value, up_value = (
        lax.psum_scatter(
            jnp.dot(features_mid, gate_weight, preferred_element_type=jnp.float32),
            "row",
            scatter_dimension=1,
            tiled=True,
        ),
        lax.psum_scatter(
            jnp.dot(features_mid, up_weight, preferred_element_type=jnp.float32),
            "row",
            scatter_dimension=1,
            tiled=True,
        ),
    )
    activated, gelu_pullback = jax.vjp(partial(jax.nn.gelu, approximate=True), gate_value)
    product_low = (activated * up_value).astype(jnp.bfloat16)
    hidden_wide = gather_hidden(product_low)
    branch_ffn = partial_cols(jnp.dot(hidden_wide, down_weight, preferred_element_type=jnp.float32))
    ffn_normed, scale_out = norm_forward(branch_ffn, forward_out_gain)
    output = (hidden_state + ffn_normed).astype(jnp.bfloat16)
    upstream = cotangent.astype(jnp.float32)
    ffn_grad, forward_out_grad = norm_backward(branch_ffn, scale_out, forward_out_gain, upstream)
    ffn_grad_wide = gather_features(ffn_grad.astype(jnp.bfloat16))
    down_weight_grad = jnp.einsum(
        "tf,td->fd", hidden_wide, ffn_grad_wide, preferred_element_type=jnp.float32
    )
    product_grad = partial_rows(
        jnp.einsum("td,fd->tf", ffn_grad_wide, down_weight, preferred_element_type=jnp.float32)
    )
    gate_grad = gelu_pullback(product_grad * up_value)[0].astype(jnp.bfloat16)
    up_grad = (product_grad * activated).astype(jnp.bfloat16)
    gate_grad_wide, up_grad_wide = (
        lax.all_gather(gate_grad, "row", axis=1, tiled=True),
        lax.all_gather(up_grad, "row", axis=1, tiled=True),
    )
    gate_weight_grad = jnp.einsum(
        "td,tf->df", features_mid, gate_grad_wide, preferred_element_type=jnp.float32
    )
    up_weight_grad = jnp.einsum(
        "td,tf->df", features_mid, up_grad_wide, preferred_element_type=jnp.float32
    )
    mid_part = jnp.einsum(
        "tf,df->td", gate_grad_wide, gate_weight, preferred_element_type=jnp.float32
    ) + jnp.einsum("tf,df->td", up_grad_wide, up_weight, preferred_element_type=jnp.float32)
    mid_grad = partial_cols(mid_part)
    state_part, forward_in_grad = norm_backward(hidden_state, scale_mid, forward_in_gain, mid_grad)
    state_grad = upstream + state_part
    attn_grad, attend_out_grad = norm_backward(branch_attn, scale_attn, attend_out_gain, state_grad)
    attn_grad_wide = gather_features(attn_grad.astype(jnp.bfloat16))
    out_weight_grad = jnp.einsum(
        "tf,td->fd", heads_wide, attn_grad_wide, preferred_element_type=jnp.float32
    )
    heads_grad = partial_rows(
        jnp.einsum("td,fd->tf", attn_grad_wide, out_weight, preferred_element_type=jnp.float32)
    )
    heads_grad = heads_grad.astype(jnp.bfloat16).reshape(sequences, LEN, HEAD_DIM)
    query_back, key_back, value_back = attend_back(
        query_rows, key_rows, value_rows, log_total, heads_grad
    )
    query_raw_grad, query_gain_part = query_pullback(query_back)
    key_normed_grad = key_turn_pullback(key_back)[0]
    key_total, value_total, query_gain_grad = (
        lax.psum(key_normed_grad.astype(jnp.bfloat16), ("row", "col")).astype(jnp.float32),
        lax.psum(value_back.astype(jnp.bfloat16), ("row", "col")).astype(jnp.float32),
        lax.psum(query_gain_part.astype(jnp.bfloat16), ("row", "col")).astype(jnp.float32),
    )
    key_raw_grad, key_gain_grad = key_norm_pullback(key_total)
    keyval_grad = (
        jnp.concatenate([key_raw_grad, value_total], axis=-1)
        .reshape(tokens, 2 * HEAD_DIM)
        .astype(jnp.bfloat16)
    )
    query_grad_wide = gather_hidden(query_raw_grad.reshape(tokens, HEAD_DIM).astype(jnp.bfloat16))
    query_weight_grad = jnp.einsum(
        "td,tf->df", features_in, query_grad_wide, preferred_element_type=jnp.float32
    )
    keyval_weight_grad = jnp.einsum(
        "td,tf->df", features_in, keyval_grad, preferred_element_type=jnp.float32
    )
    in_part = jnp.einsum(
        "tf,df->td", query_grad_wide, query_weight, preferred_element_type=jnp.float32
    ) + jnp.einsum("tf,df->td", keyval_grad, keyval_weight, preferred_element_type=jnp.float32) * (
        1.0 / lax.axis_size("col")
    )
    in_grad = partial_cols(in_part)
    residual_part, attend_in_grad = norm_backward(residual, scale_in, attend_in_gain, in_grad)
    input_grad = state_grad + residual_part
    (
        query_weight_grad,
        keyval_weight_grad,
        out_weight_grad,
        gate_weight_grad,
        up_weight_grad,
        down_weight_grad,
        attend_in_grad,
        attend_out_grad,
        forward_in_grad,
        forward_out_grad,
        query_gain_grad,
        key_gain_grad,
    ) = lax.psum(
        (
            query_weight_grad,
            keyval_weight_grad,
            out_weight_grad,
            gate_weight_grad,
            up_weight_grad,
            down_weight_grad,
            attend_in_grad,
            attend_out_grad,
            forward_in_grad,
            forward_out_grad,
            query_gain_grad,
            key_gain_grad,
        ),
        "dp",
    )
    return (
        output,
        input_grad,
        query_weight_grad,
        keyval_weight_grad,
        out_weight_grad,
        gate_weight_grad,
        up_weight_grad,
        down_weight_grad,
        attend_in_grad,
        attend_out_grad,
        forward_in_grad,
        forward_out_grad,
        query_gain_grad,
        key_gain_grad,
    )


def solution(mesh):
    placed = (
        P("dp", ("row", "col")),
        P("dp", ("row", "col")),
        P("row", "col"),
        P("row", None),
        P("col", "row"),
        P("row", "col"),
        P("row", "col"),
        P("col", "row"),
        P(("row", "col")),
        P(("row", "col")),
        P(("row", "col")),
        P(("row", "col")),
        P(),
        P(),
    )
    return jax.shard_map(
        per_device,
        mesh=mesh,
        in_specs=placed,
        out_specs=(
            P("dp", ("row", "col")),
            P("dp", ("row", "col")),
            P("row", "col"),
            P("row", None),
            P("col", "row"),
            P("row", "col"),
            P("row", "col"),
            P("col", "row"),
            P(("row", "col")),
            P(("row", "col")),
            P(("row", "col")),
            P(("row", "col")),
            P(),
            P(),
        ),
        check_vma=False,
    )
```

profile of v0, /device:TPU:0, one launch (start us, length us, event | category | flops | bytes accessed | tf_op | source)
XLA Modules:
  0.0 2345.0 jit_solution(9352799738359121478)
XLA Ops:
  9.6 12.7 psum.168
  25.7 11.7 all-gather.11.cloned.1.call-done
  37.5 7.4 fusion.91
  46.6 7.1 fusion.90
  55.5 188.7 %all-reduce.13.cloned.1.call-done = f32[4096,512]{1,0:T(8,128)} async-done(((f32[4096,512]{1,0:T(8,128)}), f32[4096,512]{1,0:T(8,128)}) %all-reduce.13.cloned.1.call-update) | async-done | bytes 8388624 | tf_op jit(solution)/shard_map/psum | solution.py:187
  253.1 93.1 %reduce-scatter.10.cloned.1.call-done = f32[4096,256]{1,0:T(8,128)} async-done(((f32[4096,512]{1,0:T(8,128)}), f32[4096,256]{1,0:T(8,128)}) %reduce-scatter.10.cloned.1.call-update) | async-done | bytes 4194320 | tf_op jit(solution)/shard_map/reduce_scatter | solution.py:28
  351.9 8.8 subtract_convert_fusion
  364.3 72.5 %while.32 = (s32[]{:T(128)}, bf16[8,1,512,256]{3,2,1,0:T(8,128)(2,1)}, f32[8,1,512,1]{2,3,1,0:T(1,128)S(1)}, s32[8]{0:T(128)S(1)}, bf16[1,4096,256]{2,1,0:T(8,12...) while((s32[]{:T(128)}, bf16[8,1,512,256]{3,2,1,0:T(8,128)(2,1)}, ...), condition=%wide.region_9.10_spmd.clone, body=%wide.region_6.9_spmd.sunk.clone | while | flops 543165440 | bytes 8161480 | solution.py:112
  436.8 56.8 %all-gather.13.cloned.1.call-done = bf16[4096,512]{1,0:T(8,128)(2,1)} async-done(((bf16[4096,256]{1,0:T(8,128)(2,1)}), bf16[4096,512]{1,0:T(8,128)(2,1)}) %all-gather.13.cloned.1.call-update) | async-done | bytes 4194320 | tf_op jit(solution)/shard_map/all_gather | solution.py:32
  493.6 6.0 fusion.92
  500.4 12.7 reduce-scatter.12.cloned.1.call-done
  515.0 11.6 psum.170
  529.4 10.1 psum.171
  541.3 11.3 all-gather.15.cloned.1.call-done
  552.6 12.2 fusion.94
  564.9 12.6 fusion.93
  577.5 177.7 %reduce-scatter.16.cloned.1.call-done = f32[4096,512]{1,0:T(8,128)} async-done(((f32[4096,1024]{1,0:T(8,128)}), f32[4096,512]{1,0:T(8,128)}) %reduce-scatter.16.cloned.1.call-update) | async-done | bytes 8388624 | tf_op jit(solution)/shard_map/reduce_scatter | solution.py:220
  755.3 191.6 %reduce-scatter.14.cloned.1.call-done = f32[4096,512]{1,0:T(8,128)} async-done(((f32[4096,1024]{1,0:T(8,128)}), f32[4096,512]{1,0:T(8,128)}) %reduce-scatter.14.cloned.1.call-update) | async-done | bytes 8388624 | tf_op jit(solution)/shard_map/reduce_scatter | solution.py:214
  946.8 8.6 multiply_convert_fusion.2
  956.0 103.7 %all-gather.17.cloned.1.call-done = bf16[4096,1024]{1,0:T(8,128)(2,1)} async-done(((bf16[4096,512]{1,0:T(8,128)(2,1)}), bf16[4096,1024]{1,0:T(8,128)(2,1)}) %all-gather.17.cloned.1.call-update) | async-done | bytes 8388624 | tf_op jit(solution)/shard_map/all_gather | solution.py:32
  1059.6 10.8 fusion.95
  1071.2 12.7 reduce-scatter.18.cloned.1.call-done
  1085.8 11.6 psum.172
  1101.0 10.1 psum.173
  1115.8 11.6 all-gather.19.cloned.1.call-done
  1127.4 9.9 fusion.96
  1137.4 190.4 %reduce-scatter.20.cloned.1.call-done = f32[4096,512]{1,0:T(8,128)} async-done(((f32[4096,1024]{1,0:T(8,128)}), f32[4096,512]{1,0:T(8,128)}) %reduce-scatter.20.cloned.1.call-update) | async-done | bytes 8388624 | tf_op jit(solution)/shard_map/reduce_scatter | solution.py:28
  1327.8 14.9 multiply_convert_fusion.1
  1343.6 103.4 %all-gather.21.cloned.1.call-done = bf16[4096,1024]{1,0:T(8,128)(2,1)} async-done(((bf16[4096,512]{1,0:T(8,128)(2,1)}), bf16[4096,1024]{1,0:T(8,128)(2,1)}) %all-gather.21.cloned.1.call-update) | async-done | bytes 8388624 | tf_op jit(solution)/shard_map/all_gather | solution.py:245
  1446.9 10.8 fusion.97
  1457.8 94.6 %all-gather.23.cloned.1.call-done = bf16[4096,1024]{1,0:T(8,128)(2,1)} async-done(((bf16[4096,512]{1,0:T(8,128)(2,1)}), bf16[4096,1024]{1,0:T(8,128)(2,1)}) %all-gather.23.cloned.1.call-update) | async-done | bytes 8388624 | tf_op jit(solution)/shard_map/all_gather | solution.py:246
  1552.4 10.4 convolution_add_fusion
  1562.9 13.3 reduce-scatter.22.cloned.1.call-done
  1579.4 11.6 psum.174
  1596.5 10.1 psum.175
  1610.9 11.6 all-gather.25.cloned.1.call-done
  1622.5 7.4 fusion.98
  1630.1 100.3 %reduce-scatter.24.cloned.1.call-done = f32[4096,256]{1,0:T(8,128)} async-done(((f32[4096,512]{1,0:T(8,128)}), f32[4096,256]{1,0:T(8,128)}) %reduce-scatter.24.cloned.1.call-update) | async-done | bytes 4194320 | tf_op jit(solution)/shard_map/reduce_scatter | solution.py:28
  1739.2 187.0 %while.33 = (s32[]{:T(128)}, f32[1,4608,256]{2,1,0:T(8,128)}, f32[1,4608,256]{2,1,0:T(8,128)}, f32[8,1,512,256]{3,2,1,0:T(8,128)}, s32[8]{0:T(128)S(1)}, /*index...) while((s32[]{:T(128)}, f32[1,4608,256]{2,1,0:T(8,128)}, ...), condition=%wide.region_31.32_spmd.clone, body=%wide.region_29.31_spmd.sunk.clone | while | flops 1349520384 | bytes 27287808 | solution.py:159
  1932.7 9.6 multiply_add_fusion.1
  1952.5 77.1 %all-reduce.17.cloned.1.call-done = (bf16[1,4096,256]{2,1,0:T(8,128)(2,1)}, bf16[1,4096,256]{2,1,0:T(8,128)(2,1)}) async-done(((bf16[1,4096,256]{2,1,0:T(8,128)(2,1)}, bf16[1,4096,256]{2,1,0:T(8,128)(2,1)}), (bf16[1,4096,256]{2,1,0:T(8,128)(2,1)}, bf16[1,4096,256]{2,1,0:T(8,128)(2,1)})) %all-reduce.17.cloned.1.call-update) | async-done | bytes 4194320 | tf_op jit(solution)/shard_map/psum | solution.py:276
  2037.8 50.3 %all-gather.27.cloned.1.call-done = bf16[1,4096,512]{2,1,0:T(8,128)(2,1)} async-done(((bf16[1,4096,256]{2,1,0:T(8,128)(2,1)}), bf16[1,4096,512]{2,1,0:T(8,128)(2,1)}) %all-gather.27.cloned.1.call-update) | async-done | bytes 4194320 | tf_op jit(solution)/shard_map/all_gather | solution.py:32
  2095.9 8.3 fusion.102
  2104.2 8.6 fusion.99
  2124.9 6.1 psum.189
  2134.1 23.2 all-reduce.6
  2157.3 10.9 psum.178
  2173.1 156.4 %all-reduce.15.cloned.1.call-done = (f32[320,512]{1,0:T(8,128)}, f32[320,512]{1,0:T(8,128)}, f32[512,320]{0,1:T(8,128)}, f32[320,1024]{1,0:T(8,128)}, f32[320,1024]{1,0:T(8,128)}, /*index=5*/f32[1024,320]{0,1:T(8,128)}) async-done(((f32[320,512]{1,0:T(8,128)}, f32[320,512]{1,0:T(8,128)}, f32[512,320]{0,1:T(8,128)}, f32[320,1024]{1,0:T(8,128)}, f32[320,1024]{1,0:T(8,128)}, /*index=5*/f32[1024,320]{0,1:T(8,128)}), ...) | async-done | bytes 5898256 | tf_op jit(solution)/shard_map/psum | solution.py:313
  (403 shorter events, 326.4 us)
Async XLA Ops:
  7.2 1052.5 %copy-start = (bf16[1024,320]{0,1:T(8,128)(2,1)S(1)}, bf16[1024,320]{0,1:T(8,128)(2,1)}, u32[]{:S(2)}) copy-start(bf16[1024,320]{0,1:T(8,128)(2,1)} %param.25) | copy-start | bytes 1966084
  7.2 30.3 %all-gather.11.cloned.1.call-start = ((), (), s32[]{:S(2)}) async-start(), calls=%async_computation.9 | async-start | bytes 3932160 | tf_op jit(solution)/shard_map/all_gather | solution.py:24
  8.0 17.7 copy-start.38
  8.0 29.5 %copy-start.26 = (bf16[320,512]{1,0:T(8,128)(2,1)S(1)}, bf16[320,512]{1,0:T(8,128)(2,1)}, u32[]{:S(2)}) copy-start(bf16[320,512]{1,0:T(8,128)(2,1)} %param.21) | copy-start | bytes 983044
  25.7 218.5 %all-reduce.13.cloned.1.call-start = ((), (), s32[]{:S(2)}) async-start(), calls=%async_computation.11 | async-start | bytes 16777216 | tf_op jit(solution)/shard_map/psum | solution.py:187
  44.9 301.2 %reduce-scatter.10.cloned.1.call-start = ((), (), s32[]{:S(2)}) async-start(), calls=%async_computation.10 | async-start | bytes 12582912 | tf_op jit(solution)/shard_map/reduce_scatter | solution.py:28
  53.7 439.9 %all-gather.13.cloned.1.call-start = ((), (), s32[]{:S(2)}) async-start(), calls=%async_computation.12 | async-start | bytes 6291456 | tf_op jit(solution)/shard_map/all_gather | solution.py:32
  54.0 296.5 %copy-start.45 = (f32[128]{0:T(128)}, f32[128]{0:T(128)S(1)}, u32[]{:S(2)}) copy-start(f32[128]{0:T(128)S(1)} %negate_power_fusion) | copy-start | bytes 1540
  55.5 294.2 %copy-start.42 = (f32[256]{0:T(256)}, f32[256]{0:T(256)S(1)}, u32[]{:S(2)}) copy-start(f32[256]{0:T(256)S(1)} %broadcast_add_fusion.1) | copy-start | bytes 3076
  55.5 194.6 %copy-start.40 = (f32[256]{0:T(256)}, f32[256]{0:T(256)S(1)}, u32[]{:S(2)}) copy-start(f32[256]{0:T(256)S(1)} %broadcast_add_fusion) | copy-start | bytes 3076
  244.2 4.6 copy-start.4
  364.3 129.4 %copy-start.18 = (bf16[512,320]{0,1:T(8,128)(2,1)S(1)}, bf16[512,320]{0,1:T(8,128)(2,1)}, u32[]{:S(2)}) copy-start(bf16[512,320]{0,1:T(8,128)(2,1)} %param.22) | copy-start | bytes 983044
  436.7 63.0 %copy-start.10 = (bf16[1,4608,256]{2,1,0:T(8,128)(2,1)}, bf16[1,4608,256]{2,1,0:T(8,128)(2,1)S(1)}, u32[]{:S(2)}) copy-start(bf16[1,4608,256]{2,1,0:T(8,128)(2,1)S(1)} %get-tuple-element.608) | copy-start | bytes 7077892
  436.8 76.3 %reduce-scatter.12.cloned.1.call-start = ((), (), s32[]{:S(2)}) async-start(), calls=%async_computation.13 | async-start | bytes 7864320 | tf_op jit(solution)/shard_map/reduce_scatter | solution.py:36
  499.7 52.9 %all-gather.15.cloned.1.call-start = ((), (), s32[]{:S(2)}) async-start(), calls=%async_computation.14 | async-start | bytes 3932160 | tf_op jit(solution)/shard_map/all_gather | solution.py:24
  541.0 214.3 %reduce-scatter.16.cloned.1.call-start = ((), (), s32[]{:S(2)}) async-start(), calls=%async_computation.16 | async-start | bytes 25165824 | tf_op jit(solution)/shard_map/reduce_scatter | solution.py:220
  564.8 382.0 %reduce-scatter.14.cloned.1.call-start = ((), (), s32[]{:S(2)}) async-start(), calls=%async_computation.15 | async-start | bytes 25165824 | tf_op jit(solution)/shard_map/reduce_scatter | solution.py:214
  577.5 482.2 %all-gather.17.cloned.1.call-start = ((), (), s32[]{:S(2)}) async-start(), calls=%async_computation.17 | async-start | bytes 12582912 | tf_op jit(solution)/shard_map/all_gather | solution.py:32
  955.5 128.4 %reduce-scatter.18.cloned.1.call-start = ((), (), s32[]{:S(2)}) async-start(), calls=%async_computation.18 | async-start | bytes 7864320 | tf_op jit(solution)/shard_map/reduce_scatter | solution.py:36
  1070.5 56.9 %all-gather.19.cloned.1.call-start = ((), (), s32[]{:S(2)}) async-start(), calls=%async_computation.19 | async-start | bytes 3932160 | tf_op jit(solution)/shard_map/all_gather | solution.py:24
  1115.7 212.0 %reduce-scatter.20.cloned.1.call-start = ((), (), s32[]{:S(2)}) async-start(), calls=%async_computation.20 | async-start | bytes 25165824 | tf_op jit(solution)/shard_map/reduce_scatter | solution.py:28
  1137.3 309.6 %all-gather.21.cloned.1.call-start = ((), (), s32[]{:S(2)}) async-start(), calls=%async_computation.21 | async-start | bytes 12582912 | tf_op jit(solution)/shard_map/all_gather | solution.py:245
  1342.7 104.2 %copy-start.24 = (bf16[320,1024]{1,0:T(8,128)(2,1)S(1)}, bf16[320,1024]{1,0:T(8,128)(2,1)}, u32[]{:S(2)}) copy-start(bf16[320,1024]{1,0:T(8,128)(2,1)} %param.23) | copy-start | bytes 1966084
  1342.8 209.6 %all-gather.23.cloned.1.call-start = ((), (), s32[]{:S(2)}) async-start(), calls=%async_computation.22 | async-start | bytes 12582912 | tf_op jit(solution)/shard_map/all_gather | solution.py:246
  1343.3 232.8 %reduce-scatter.22.cloned.1.call-start = ((), (), s32[]{:S(2)}) async-start(), calls=%async_computation.23 | async-start | bytes 7864320 | tf_op jit(solution)/shard_map/reduce_scatter | solution.py:36
  1562.8 59.7 %all-gather.25.cloned.1.call-start = ((), (), s32[]{:S(2)}) async-start(), calls=%async_computation.24 | async-start | bytes 3932160 | tf_op jit(solution)/shard_map/all_gather | solution.py:24
  1606.6 15.9 copy-start.19
  1610.8 119.6 %reduce-scatter.24.cloned.1.call-start = ((), (), s32[]{:S(2)}) async-start(), calls=%async_computation.25 | async-start | bytes 12582912 | tf_op jit(solution)/shard_map/reduce_scatter | solution.py:28
  1629.9 399.8 %all-reduce.17.cloned.1.call-start = ((), (), s32[]{:S(2)}) async-start(), calls=%async_computation.29 | async-start | bytes 8388608 | tf_op jit(solution)/shard_map/psum | solution.py:276
  1926.2 6.4 slice-start
  1926.2 6.4 slice-start.1
  1943.8 144.3 %all-gather.27.cloned.1.call-start = ((), (), s32[]{:S(2)}) async-start(), calls=%async_computation.27 | async-start | bytes 6291456 | tf_op jit(solution)/shard_map/all_gather | solution.py:32
  1944.5 4.8 copy-start.6
  1949.3 80.4 %copy-start.31 = (f32[4096]{0:T(1024)S(1)}, f32[4096]{0:T(1024)}, u32[]{:S(2)}) copy-start(f32[4096]{0:T(1024)} %copy-done.30) | copy-start | bytes 49156
  1949.3 80.4 %copy-start.41 = (f32[256]{0:T(256)S(1)}, f32[256]{0:T(256)}, u32[]{:S(2)}) copy-start(f32[256]{0:T(256)} %copy-done.40) | copy-start | bytes 3076
  1952.5 178.5 %reduce-scatter.26.cloned.1.call-start = ((), (), s32[]{:S(2)}) async-start(), calls=%async_computation.26 | async-start | bytes 7864320 | tf_op jit(solution)/shard_map/reduce_scatter | solution.py:36
  2033.6 54.5 %copy-start.20 = (bf16[320,512]{1,0:T(8,128)(2,1)S(1)}, bf16[320,512]{1,0:T(8,128)(2,1)}, u32[]{:S(2)}) copy-start(bf16[320,512]{1,0:T(8,128)(2,1)} %param.20) | copy-start | bytes 983044
  2037.8 54.2 %copy-start.16 = (bf16[1,4096,256]{2,1,0:T(8,128)(2,1)}, bf16[1,4096,256]{2,1,0:T(8,128)(2,1)S(1)}, u32[]{:S(2)}) copy-start(bf16[1,4096,256]{2,1,0:T(8,128)(2,1)S(1)} %fusion.55) | copy-start | bytes 6291460
  2037.8 54.2 %copy-start.27 = (bf16[320,512]{1,0:T(8,128)(2,1)S(1)}, bf16[320,512]{1,0:T(8,128)(2,1)}, u32[]{:S(2)}) copy-start(bf16[320,512]{1,0:T(8,128)(2,1)} %param.21) | copy-start | bytes 983044
  2095.6 8.6 copy-start.11
  2095.6 233.9 %all-reduce.15.cloned.1.call-start = ((), (), s32[]{:S(2)}) async-start(), calls=%async_computation.28 | async-start | bytes 11796480 | tf_op jit(solution)/shard_map/psum | solution.py:313
  2095.9 16.9 slice-start.2
  2104.2 8.6 slice-start.3
  2124.8 6.2 copy-start.5
  2124.8 6.2 copy-start.29
  2124.8 6.2 copy-start.39
  2124.8 9.2 copy-start.44
  2329.5 5.0 copy-start.23
  (31 other events, 72.9 us)
Sparse Core Ops, SparseCore 0:
  25.8 11.6 all-gather.10
  45.0 199.1 all-reduce.12
  246.5 99.5 reduce-scatter.9
  436.9 56.7 all-gather.12
  499.8 13.1 reduce-scatter.11
  541.1 11.4 all-gather.14
  564.9 190.2 reduce-scatter.15
  757.7 189.1 reduce-scatter.13
  955.6 104.0 all-gather.16
  1070.6 13.1 reduce-scatter.17
  1115.9 11.4 all-gather.18
  1137.4 190.2 reduce-scatter.19
  1342.9 104.0 all-gather.20
  1448.3 104.0 all-gather.22
  1562.9 13.1 reduce-scatter.21
  1611.0 11.4 all-gather.24
  1630.0 100.4 reduce-scatter.23
  1943.9 85.6 all-reduce.16
  2031.3 56.8 all-gather.26
  2095.7 13.1 reduce-scatter.25
  2125.0 204.4 all-reduce.14
where the time goes:
time: 2350 us; the launch traced here: 2340 us
  waiting for transfers between devices  1670 us (71%)
  matrix products  236 us (10%)
  other arithmetic  136 us (6%)
  blocking collectives  118 us (5%)
  local copies, waits for them, and re-layouts  105 us (4%)
  loops' own time  62.7 us (3%)
    reduce_scatter x3, waiting for transfers between devices, partial_rows(): return lax.psum_scatter(values, 'row', scatter_dimension=1, tiled=True)  384 us
    all_gather x3, waiting for transfers between devices, gather_hidden(): return lax.all_gather(values, 'row', axis=1, tiled=True)  211 us
    reduce_scatter x1, waiting for transfers between devices, per_device(): lax.psum_scatter(jnp.dot(features_mid, gate_weight, preferred_element_typ...  192 us
    psum x1, waiting for transfers between devices, per_device(): lax.psum(jnp.dot(features_in, keyval_weight, preferred_element_type=jnp.f...  189 us
    reduce_scatter x1, waiting for transfers between devices, per_device(): lax.psum_scatter(jnp.dot(features_mid, up_weight, preferred_element_type=...  178 us
    psum x1, waiting for transfers between devices, per_device(): lax.psum((query_weight_grad, keyval_weight_grad, out_weight_grad, gate_we...  156 us
    all_gather x1, waiting for transfers between devices, per_device(): lax.all_gather(gate_grad, 'row', axis=1, tiled=True)  103 us
    all_gather x1, waiting for transfers between devices, per_device(): lax.all_gather(up_grad, 'row', axis=1, tiled=True)  94.6 us
  transfers between devices with their start and end apart: 21, of which 20 were waited for; matrix products, arithmetic and copies ran while one was open for 4% of the time, Pallas kernels for 0%

commit v1 on v0

v1 whole, which is shorter than its diff:
```python
from functools import partial

import jax
import jax.numpy as jnp
from jax import lax
from jax.experimental import pallas as pl
from jax.experimental.pallas import tpu as pltpu
from jax.sharding import PartitionSpec as P

D = 640
HEADS = 4
HEAD_DIM = 256
WINDOW = 512
LEN = 4096
PARTS = 4
BLOCK = 256
SPAN = BLOCK + WINDOW

EPSILON = 1e-06
ROPE_BASE = 10000.0

F32 = jnp.float32
BF16 = jnp.bfloat16


def swap(values, axis):
    return lax.ppermute(values, axis, [(0, 1), (1, 0)])


def swap_dp(values, bit):
    size = lax.axis_size("dp")
    return lax.ppermute(values, "dp", [(i, i ^ bit) for i in range(size)])


def ordered(flag, own, other, axis):
    first = jnp.where(flag == 0, own, other)
    second = jnp.where(flag == 0, other, own)
    return jnp.concatenate([first, second], axis=axis)


def exchange(blocks, part):
    got = [lax.dynamic_index_in_dim(blocks, part, 0, keepdims=False)]
    for k in (1, 2, 3):
        sent = lax.dynamic_index_in_dim(blocks, part ^ k, 0, keepdims=False)
        got.append(lax.ppermute(sent, ("row", "col"), [(i, i ^ k) for i in range(PARTS)]))
    return got


def to_tokens(values, part, col):
    tokens = values.shape[0] // PARTS
    got = exchange(values.reshape(PARTS, tokens, values.shape[1]), part)
    return jnp.concatenate(
        [ordered(col, got[0], got[1], 1), ordered(col, got[2], got[3], 1)], axis=1
    )


def to_features(values, part, col):
    tokens = values.shape[0]
    width = values.shape[1] // PARTS
    quarters = [values[:, i * width : (i + 1) * width] for i in range(PARTS)]
    own = [jnp.where(col == 0, quarters[0], quarters[1]), jnp.where(col == 0, quarters[1], quarters[0])]
    far = [jnp.where(col == 0, quarters[2], quarters[3]), jnp.where(col == 0, quarters[3], quarters[2])]
    sent = own + far
    got = [sent[0]]
    for k in (1, 2, 3):
        got.append(lax.ppermute(sent[k], ("row", "col"), [(i, i ^ k) for i in range(PARTS)]))
    out = jnp.zeros((PARTS, tokens, width), values.dtype)
    for k in range(PARTS):
        out = lax.dynamic_update_index_in_dim(out, got[k], part ^ k, 0)
    return out.reshape(PARTS * tokens, width)


def gather_gains(gains, col):
    half = ordered(col, gains, swap(gains, "col"), 1)
    return jnp.concatenate([half, swap(half, "row")], axis=1)


def gather_weight(shard):
    tall = jnp.concatenate([shard, swap(shard, "row")], axis=0)
    return jnp.concatenate([tall, swap(tall, "col")], axis=1)


def reduce_gradient(grad):
    rows, cols = grad.shape
    low = grad.astype(BF16)
    half = grad[:, : cols // 2] + swap(low[:, cols // 2 :], "col").astype(F32)
    low = half[rows // 2 :].astype(BF16)
    total = half[: rows // 2] + swap(low, "row").astype(F32)
    return all_reduce_dp(total)


def all_reduce_dp(total):
    size = lax.axis_size("dp")
    me = lax.axis_index("dp")
    bit = 1
    steps = []
    while bit < size:
        axis = 1 if total.shape[1] % 256 == 0 else 0
        length = total.shape[axis] // 2
        mine = (me // bit) % 2
        keep = lax.dynamic_slice_in_dim(total, mine * length, length, axis)
        send = lax.dynamic_slice_in_dim(total, (1 - mine) * length, length, axis)
        total = keep + swap_dp(send.astype(BF16), bit).astype(F32)
        steps.append((bit, axis, mine))
        bit *= 2
    result = total.astype(BF16)
    for bit, axis, mine in reversed(steps):
        result = ordered(mine, result, swap_dp(result, bit), axis)
    return result.astype(F32)


def scale_of(values):
    return lax.rsqrt(jnp.mean(values * values, axis=-1, keepdims=True) + EPSILON)


def norm_backward(values, scale, offset, gradient):
    unit = values * scale
    scaled = gradient * (1.0 + offset)
    inner = jnp.mean(scaled * unit, axis=-1, keepdims=True)
    return scale * (scaled - unit * inner), jnp.sum(gradient * unit, axis=0)


def rms_scale(values, offset):
    return values * scale_of(values) * (1.0 + offset)


def rotate(values, cosine, sine):
    half_dim = values.shape[-1] // 2
    first_half = values[..., :half_dim]
    second_half = values[..., half_dim:]
    return jnp.concatenate(
        [first_half * cosine - second_half * sine, second_half * cosine + first_half * sine],
        axis=-1,
    )


def rope_tables(first, count):
    half_dim = HEAD_DIM // 2
    frequency = ROPE_BASE ** (-(jnp.arange(half_dim, dtype=F32) * 2.0 / HEAD_DIM))
    angles = (first + jnp.arange(count, dtype=jnp.int32)).astype(F32)[:, None] * frequency[None, :]
    return (jnp.cos(angles), jnp.sin(angles))


def nn(a, b):
    return jnp.dot(a, b, preferred_element_type=F32)


def nt(a, b):
    return lax.dot_general(a, b, (((1,), (1,)), ((), ())), preferred_element_type=F32)


def tn(a, b):
    return lax.dot_general(a, b, (((0,), (0,)), ((), ())), preferred_element_type=F32)


def seen_mask(first_key):
    key = lax.broadcasted_iota(jnp.int32, (SPAN, BLOCK), 0)
    query = lax.broadcasted_iota(jnp.int32, (SPAN, BLOCK), 1)
    return (key > query) & (key <= query + WINDOW) & (key >= first_key)


def attend_kernel(first_ref, query_ref, key_ref, value_ref, out_ref):
    block = pl.program_id(0)
    start = pl.multiple_of(block * BLOCK, BLOCK)
    keys = key_ref[pl.ds(start, SPAN), :]
    values = value_ref[pl.ds(start, SPAN), :]
    mask = seen_mask(first_ref[0] - start)
    for head in range(HEADS):
        columns = slice(head * HEAD_DIM, (head + 1) * HEAD_DIM)
        scores = nt(keys, query_ref[:, columns])
        weights = jnp.where(mask, jnp.exp(scores), 0.0)
        total = jnp.sum(weights, axis=0, keepdims=True)
        probs = (weights * (1.0 / total)).astype(BF16)
        out_ref[:, columns] = tn(probs, values).astype(BF16)


def attend_back_kernel(first_ref, query_ref, key_ref, value_ref, grad_ref, query_out, key_out, value_out):
    block = pl.program_id(0)
    start = pl.multiple_of(block * BLOCK, BLOCK)
    window = pl.ds(start, SPAN)
    keys = key_ref[window, :]
    values = value_ref[window, :]
    mask = seen_mask(first_ref[0] - start)

    @pl.when(block == 0)
    def _():
        key_out[...] = jnp.zeros_like(key_out)
        value_out[...] = jnp.zeros_like(value_out)

    key_sum = key_out[window, :]
    value_sum = value_out[window, :]
    for head in range(HEADS):
        columns = slice(head * HEAD_DIM, (head + 1) * HEAD_DIM)
        queries = query_ref[:, columns]
        grads = grad_ref[:, columns]
        weights = jnp.where(mask, jnp.exp(nt(keys, queries)), 0.0)
        probs = weights * (1.0 / jnp.sum(weights, axis=0, keepdims=True))
        prob_grad = nt(values, grads)
        inner = jnp.sum(prob_grad * probs, axis=0, keepdims=True)
        score_grad = (probs * (prob_grad - inner)).astype(BF16)
        query_out[:, columns] = tn(score_grad, keys)
        key_sum += nn(score_grad, queries)
        value_sum += nn(probs.astype(BF16), grads)
    key_out[window, :] = key_sum
    value_out[window, :] = value_sum


def attend(first, query_rows, keys, values):
    tokens, width = query_rows.shape
    span = keys.shape[0]
    return pl.pallas_call(
        attend_kernel,
        grid=(tokens // BLOCK,),
        in_specs=[
            pl.BlockSpec(memory_space=pltpu.SMEM),
            pl.BlockSpec((BLOCK, width), lambda i: (i, 0)),
            pl.BlockSpec((span, HEAD_DIM), lambda i: (0, 0)),
            pl.BlockSpec((span, HEAD_DIM), lambda i: (0, 0)),
        ],
        out_specs=pl.BlockSpec((BLOCK, width), lambda i: (i, 0)),
        out_shape=jax.ShapeDtypeStruct((tokens, width), BF16),
        compiler_params=pltpu.CompilerParams(vmem_limit_bytes=32 << 20),
        cost_estimate=pl.CostEstimate(
            flops=4 * tokens * width * SPAN, bytes_accessed=4 * tokens * width + 4 * span * HEAD_DIM, transcendentals=tokens * HEADS * SPAN
        ),
        name="attend",
    )(first, query_rows, keys, values)


def attend_back(first, query_rows, keys, values, heads_grad):
    tokens, width = query_rows.shape
    span = keys.shape[0]
    return pl.pallas_call(
        attend_back_kernel,
        grid=(tokens // BLOCK,),
        in_specs=[
            pl.BlockSpec(memory_space=pltpu.SMEM),
            pl.BlockSpec((BLOCK, width), lambda i: (i, 0)),
            pl.BlockSpec((span, HEAD_DIM), lambda i: (0, 0)),
            pl.BlockSpec((span, HEAD_DIM), lambda i: (0, 0)),
            pl.BlockSpec((BLOCK, width), lambda i: (i, 0)),
        ],
        out_specs=[
            pl.BlockSpec((BLOCK, width), lambda i: (i, 0)),
            pl.BlockSpec((span, HEAD_DIM), lambda i: (0, 0)),
            pl.BlockSpec((span, HEAD_DIM), lambda i: (0, 0)),
        ],
        out_shape=[
            jax.ShapeDtypeStruct((tokens, width), F32),
            jax.ShapeDtypeStruct((span, HEAD_DIM), F32),
            jax.ShapeDtypeStruct((span, HEAD_DIM), F32),
        ],
        compiler_params=pltpu.CompilerParams(vmem_limit_bytes=32 << 20),
        cost_estimate=pl.CostEstimate(
            flops=10 * tokens * width * SPAN, bytes_accessed=8 * tokens * width + 12 * span * HEAD_DIM, transcendentals=tokens * HEADS * SPAN
        ),
        name="attend_back",
    )(first, query_rows, keys, values, heads_grad)


def per_device(
    inputs,
    cotangent,
    query_weight,
    keyval_weight,
    out_weight,
    gate_weight,
    up_weight,
    down_weight,
    attend_in_gain,
    attend_out_gain,
    forward_in_gain,
    forward_out_gain,
    query_gain,
    key_gain,
):
    assert inputs.shape[0] == LEN
    row = lax.axis_index("row")
    col = lax.axis_index("col")
    part = row * 2 + col
    tokens = LEN // PARTS
    ahead = [(i, i + 1) for i in range(PARTS - 1)]
    behind = [(i + 1, i) for i in range(PARTS - 1)]

    residual_low = to_tokens(inputs, part, col)
    keyval_full = jnp.concatenate([keyval_weight, swap(keyval_weight, "row")], axis=0)
    query_full = gather_weight(query_weight)
    gains = jnp.stack([attend_in_gain, attend_out_gain, forward_in_gain, forward_out_gain])
    gains = gather_gains(gains, col)
    attend_in_gain, attend_out_gain, forward_in_gain, forward_out_gain = (gains[i] for i in range(4))
    out_full = gather_weight(out_weight.T)
    gate_full = gather_weight(gate_weight)
    up_full = gather_weight(up_weight)
    down_full = gather_weight(down_weight.T)
    upstream = to_tokens(cotangent, part, col).astype(F32)

    cosine, sine = rope_tables(part * tokens, tokens)
    first = jnp.where(part == 0, WINDOW, 0).astype(jnp.int32).reshape(1)

    residual = residual_low.astype(F32)
    scale_in = scale_of(residual)
    attend_in = (residual * scale_in * (1.0 + attend_in_gain)).astype(BF16)
    keyval_raw = nn(attend_in, keyval_full)
    key_raw = keyval_raw[:, :HEAD_DIM]
    value_rows = keyval_raw[:, HEAD_DIM:].astype(BF16)

    def query_prep(raw, gain):
        return rotate(rms_scale(raw, gain), cosine[:, None, :], sine[:, None, :]) * HEAD_DIM ** (-0.5)

    def key_prep(raw, gain):
        return rotate(rms_scale(raw, gain), cosine, sine)

    key_ready, key_pullback = jax.vjp(key_prep, key_raw, key_gain)
    key_rows = key_ready.astype(BF16)
    halo = lax.ppermute(
        jnp.concatenate([key_rows[tokens - WINDOW :], value_rows[tokens - WINDOW :]], axis=1),
        ("row", "col"),
        ahead,
    )
    query_raw = nn(attend_in, query_full).reshape(tokens, HEADS, HEAD_DIM)
    query_ready, query_pullback = jax.vjp(query_prep, query_raw, query_gain)
    query_rows = query_ready.astype(BF16).reshape(tokens, HEADS * HEAD_DIM)
    keys = jnp.concatenate([halo[:, :HEAD_DIM], key_rows], axis=0)
    values = jnp.concatenate([halo[:, HEAD_DIM:], value_rows], axis=0)
    mixed_heads = attend(first, query_rows, keys, values)

    branch_attn = nt(mixed_heads, out_full)
    scale_attn = scale_of(branch_attn)
    hidden_state = residual + branch_attn * scale_attn * (1.0 + attend_out_gain)
    scale_mid = scale_of(hidden_state)
    forward_in = (hidden_state * scale_mid * (1.0 + forward_in_gain)).astype(BF16)
    gate_value = nn(forward_in, gate_full)
    up_value = nn(forward_in, up_full)
    activated, gelu_pullback = jax.vjp(partial(jax.nn.gelu, approximate=True), gate_value)
    product = (activated * up_value).astype(BF16)
    branch_ffn = nt(product, down_full)
    scale_out = scale_of(branch_ffn)
    output = (hidden_state + branch_ffn * scale_out * (1.0 + forward_out_gain)).astype(BF16)
    output = to_features(output, part, col)

    ffn_grad, forward_out_grad = norm_backward(branch_ffn, scale_out, forward_out_gain, upstream)
    ffn_grad = ffn_grad.astype(BF16)
    down_grad = reduce_gradient(tn(ffn_grad, product))
    product_grad = nn(ffn_grad, down_full)
    gate_grad = gelu_pullback(product_grad * up_value)[0].astype(BF16)
    up_grad = (product_grad * activated).astype(BF16)
    gate_weight_grad = reduce_gradient(tn(forward_in, gate_grad))
    up_weight_grad = reduce_gradient(tn(forward_in, up_grad))
    mid_grad = nt(gate_grad, gate_full) + nt(up_grad, up_full)
    state_part, forward_in_grad = norm_backward(hidden_state, scale_mid, forward_in_gain, mid_grad)
    state_grad = upstream + state_part
    attn_grad, attend_out_grad = norm_backward(branch_attn, scale_attn, attend_out_gain, state_grad)
    attn_grad = attn_grad.astype(BF16)
    out_grad = reduce_gradient(tn(attn_grad, mixed_heads))
    heads_grad = nn(attn_grad, out_full).astype(BF16)
    query_back, key_back, value_back = attend_back(first, query_rows, keys, values, heads_grad)

    back = lax.ppermute(
        jnp.concatenate([key_back[:WINDOW], value_back[:WINDOW]], axis=1).astype(BF16),
        ("row", "col"),
        behind,
    ).astype(F32)
    query_raw_grad, query_gain_grad = query_pullback(query_back.reshape(tokens, HEADS, HEAD_DIM))
    query_raw_grad = query_raw_grad.reshape(tokens, HEADS * HEAD_DIM).astype(BF16)
    query_grad = tn(attend_in, query_raw_grad)
    in_query = nt(query_raw_grad, query_full)

    rest = tokens - WINDOW
    key_own = jnp.concatenate([key_back[WINDOW : WINDOW + rest], key_back[tokens:] + back[:, :HEAD_DIM]], axis=0)
    value_own = jnp.concatenate([value_back[WINDOW : WINDOW + rest], value_back[tokens:] + back[:, HEAD_DIM:]], axis=0)
    key_raw_grad, key_gain_grad = key_pullback(key_own)
    keyval_raw_grad = jnp.concatenate([key_raw_grad, value_own], axis=1).astype(BF16)
    keyval_grad = tn(attend_in, keyval_raw_grad)
    in_grad = in_query + nt(keyval_raw_grad, keyval_full)
    residual_part, attend_in_grad = norm_backward(residual, scale_in, attend_in_gain, in_grad)
    input_grad = to_features((state_grad + residual_part).astype(BF16), part, col).astype(F32)

    query_grad = reduce_gradient(query_grad)
    keyval_mine = lax.dynamic_slice_in_dim(keyval_grad, col * HEAD_DIM, HEAD_DIM, 1)
    keyval_sent = lax.dynamic_slice_in_dim(keyval_grad, (1 - col) * HEAD_DIM, HEAD_DIM, 1)
    keyval_total = reduce_gradient(jnp.concatenate([keyval_mine, keyval_sent], axis=1))
    keyval_total = ordered(col, keyval_total, swap(keyval_total, "col"), 1)

    gain_rows = jnp.concatenate(
        [attend_in_grad, attend_out_grad, forward_in_grad, forward_out_grad, query_gain_grad, key_gain_grad]
    )
    rows4 = gain_rows[: 4 * D].reshape(4, D)
    half = rows4.reshape(4, 2, 2, D // 4)
    mine = lax.dynamic_index_in_dim(half[:, 0], col, 1, keepdims=False)
    others = [
        lax.dynamic_index_in_dim(half[:, 0], 1 - col, 1, keepdims=False),
        lax.dynamic_index_in_dim(half[:, 1], col, 1, keepdims=False),
        lax.dynamic_index_in_dim(half[:, 1], 1 - col, 1, keepdims=False),
    ]
    gain_total = mine
    for k in (1, 2, 3):
        gain_total = gain_total + lax.ppermute(others[k - 1], ("row", "col"), [(i, i ^ k) for i in range(PARTS)])
    small = gain_rows[4 * D :]
    small = small + swap(small, "col")
    small = small + swap(small, "row")
    packed = jnp.concatenate([gain_total.reshape(-1), small])
    packed = lax.psum(packed, "dp")
    gain_total = packed[:D].reshape(4, D // 4)
    query_gain_grad = packed[D : D + HEAD_DIM]
    key_gain_grad = packed[D + HEAD_DIM :]
    return (
        output,
        input_grad,
        query_grad,
        keyval_total,
        out_grad.T,
        gate_weight_grad,
        up_weight_grad,
        down_grad.T,
        gain_total[0],
        gain_total[1],
        gain_total[2],
        gain_total[3],
        query_gain_grad,
        key_gain_grad,
    )


def solution(mesh):
    wide = P("dp", ("row", "col"))
    gain = P(("row", "col"))
    weights = (P("row", "col"), P("row", None), P("col", "row"), P("row", "col"), P("row", "col"), P("col", "row"))
    gains = (gain, gain, gain, gain, P(), P())
    return jax.shard_map(
        per_device,
        mesh=mesh,
        in_specs=(wide, wide) + weights + gains,
        out_specs=(wide, wide) + weights + gains,
        check_vma=False,
    )
```

time: 2350 us -> 537 us (0.23)
  waiting for transfers between devices: 1670 us -> 160 us
  matrix products: 236 us -> 84.4 us
  blocking collectives: 118 us -> 21.9 us
  starting transfers between devices: 2.44 us -> 83.7 us
  other arithmetic: 136 us -> 69.3 us
  loops' own time: 62.7 us -> 0 us
    reduce_scatter x9 -> x0, waiting for transfers between devices: 792 us -> none  [the longest x3 384 us: partial_rows(): return lax.psum_scatter(values, 'row', scatter_dimension=1, tiled=True)]
    all_gather x9 -> x0, waiting for transfers between devices: 455 us -> none  [the longest x3 211 us: gather_hidden(): return lax.all_gather(values, 'row', axis=1, tiled=True)]
    psum x3 -> x0, waiting for transfers between devices: 422 us -> none  [the longest x1 189 us: per_device(): lax.psum(jnp.dot(features_in, keyval_weight, preferred_element_type=jnp.f...]
    ppermute x0 -> x81, waiting for transfers between devices: none -> 160 us  [the longest x36 77.7 us: swap_dp(): return lax.ppermute(values, 'dp', [(i, i ^ bit) for i in range(size)])]
    dot_general x74 -> x18, matrix products: 236 us -> 84.4 us  [the longest x6 37.8 us: nn(): return jnp.dot(a, b, preferred_element_type=F32)]
    psum x10 -> x1, blocking collectives: 118 us -> 21.9 us  [per_device(): packed = lax.psum(packed, 'dp')]
    ppermute x0 -> x81, starting transfers between devices: none -> 83.7 us  [the longest x36 43.1 us: swap_dp(): return lax.ppermute(values, 'dp', [(i, i ^ bit) for i in range(size)])]
    another operation x2 -> x0, loops' own time: 62.7 us -> none  [the longest x1 31.4 us: attend_back(): lax.scan(one_block, (zero_sums, zero_sums), block_starts)]
  transfers between devices with their start and end apart: 21 -> 81, of which waited for: 20 -> 37; matrix products, arithmetic and copies ran while one was open for 4% -> 26% of each run, Pallas kernels for 0% -> 1%
where the time goes in v1:
time: 537 us; the launch traced here: 528 us
  waiting for transfers between devices  160 us (30%)
  matrix products  84.4 us (16%)
  starting transfers between devices  83.7 us (16%)
  local copies, waits for them, and re-layouts  82.9 us (15%)
  other arithmetic  69.3 us (13%)
  Pallas kernels  22.5 us (4%)
  blocking collectives  21.9 us (4%)
    ppermute x36, waiting for transfers between devices, swap_dp(): return lax.ppermute(values, 'dp', [(i, i ^ bit) for i in range(size)])  77.7 us
    ppermute x36, starting transfers between devices, swap_dp(): return lax.ppermute(values, 'dp', [(i, i ^ bit) for i in range(size)])  43.1 us
    dot_general x6, matrix products, nn(): return jnp.dot(a, b, preferred_element_type=F32)  37.8 us
    ppermute x6, waiting for transfers between devices, exchange(): lax.ppermute(sent, ('row', 'col'), [(i, i ^ k) for i in range(PARTS)])  34.9 us
    ppermute x28, waiting for transfers between devices, swap(): return lax.ppermute(values, axis, [(0, 1), (1, 0)])  30.6 us
    dot_general x6, matrix products, tn(): lax.dot_general(a, b, (((0,), (0,)), ((), ())), preferred_element_type=F32)  25 us
    unnamed x177, local copies, waits for them, and re-layouts  23.8 us
    ppermute x28, starting transfers between devices, swap(): return lax.ppermute(values, axis, [(0, 1), (1, 0)])  22.4 us
  transfers between devices with their start and end apart: 81, of which 37 were waited for; matrix products, arithmetic and copies ran while one was open for 26% of the time, Pallas kernels for 1%

profile of v1, /device:TPU:0, one launch (start us, length us, event | category | flops | bytes accessed | tf_op | source)
XLA Modules:
  0.0 527.7 jit_solution(8970491538250548473)
XLA Ops:
  0.7 3.2 reshape.227
  3.9 3.2 reshape.231
  7.2 6.4 %constant_dynamic-slice_fusion.7 = (bf16[1,1024,160]{1,0,2:T(2,128)(2,1)}, bf16[1,1024,160]{1,0,2:T(2,128)(2,1)}, bf16[1,1024,160]{1,0,2:T(2,128)(2,1)S(1)}, bf1...) fusion(bf16[4,1024,160]{1,0,2:T(4,128)(2,1)S(1)} %reshape.231, ...), kind=kLoop, calls=%fused_computation.286 | loop fusion | bytes 5242896 | tf_op jit(solution)/shard_map/jit(dynamic_index_in_dim)/dynamic_slice | solution.py:42
  31.9 9.2 %collective-permute-done.4 = f32[4,320]{1,0:T(4,128)S(1)} collective-permute-done((f32[4,320]{1,0:T(4,128)S(1)}, f32[4,320]{1,0:T(4,128)S(1)}, u32[]{:S(2)}, u32[]{:S(2)}) %collective-permute-start.4) | collective-permute-done | bytes 5152 | tf_op jit(solution)/shard_map/ppermute | solution.py:27
  45.6 5.2 collective-permute-done.2
  58.7 3.2 fusion.46
  61.9 24.6 %collective-permute-done.21 = bf16[1024,160]{0,1:T(8,128)(2,1)S(1)} collective-permute-done((bf16[1024,160]{0,1:T(8,128)(2,1)}, bf16[1024,160]{0,1:T(8,128)(2,1)S(1)}, u32[]{:S(2)}, u32[]{:S(2)}) %collective-permute-start.21) | collective-permute-done | bytes 327712 | tf_op jit(solution)/shard_map/ppermute | solution.py:45
  87.9 5.0 collective-permute-done.22
  133.2 7.0 %attend.1 = bf16[1024,1024]{1,0:T(8,128)(2,1)S(1)} custom-call(s32[1]{0:T(128)} %bitcast.4.first_ref, bf16[1024,1024]{1,0:T(8,128)(2,1)S(1)} %copy.63.query_ref, bf16[1536,256]{1,0:T(8,128)(2,1)S(1)} %maximum_maximum_fusion.1.key_ref, bf16[1536,256]{1,0:T(8,128)(2,1)S(1)} %copy-done.4), custom_call_target="tpu_custom_call" | custom-call | flops 3221225472 | bytes 5767168 | tf_op jit(solution)/shard_map/attend/pallas_call | solution.py:211
  144.1 5.7 %fusion.30 = f32[1024,2048]{1,0:T(8,128)S(1)} fusion(bf16[1024,640]{0,1:T(8,128)(2,1)S(1)} %multiply_convert_fusion.3, bf16[640,1024]{1,0:T(8,128)(2,1)} %collective-permute-done.12, bf16[640,1024]{1,0:T(8,128)(2,1)} %constant_dynamic-update-slice_fusion.4), kind=kOutput, calls=%fused_computation.73 | convolution fusion | flops 2689597440 | bytes 12320768 | tf_op jit(solution)/shard_map/dot_general | solution.py:145
  149.9 9.4 %multiply_convert_fusion.1 = (bf16[1024,2048]{1,0:T(8,128)(2,1)S(1)}, f32[1024,2048]{1,0:T(8,128)}) fusion(f32[1024,2048]{1,0:T(8,128)S(1)} %fusion.30, bf16[1024,640]{0,1:T(8,128)(2,1)S(1)} %multiply_convert_fusion.3, bf16[640,1024]{1,0:T(8,128)(2,1)} %collective-permute-done.14, bf16[640,1024]{1,0:T(8,128)(2,1)} %constant_dynamic-update-slice_fusion.6), kind=kOutput, calls=%fused_computation.10 | convolution fusion | flops 2710568960 | bytes 24903680 | tf_op jit(solution)/shard_map/dot_general | solution.py:145
  159.3 4.7 multiply_reduce_fusion.7
  165.1 3.9 fusion.17
  169.0 4.5 fusion.93
  173.5 15.3 %fusion.6 = (bf16[1024,2048]{1,0:T(8,128)(2,1)}, bf16[1024,2048]{1,0:T(8,128)(2,1)}) fusion(f32[1024,2048]{1,0:T(8,128)S(1)} %fusion.30, f32[1024,2048]{1,0:T(8,128)} %get-tuple-element.141, bf16[1024,640]{0,1:T(8,128)(2,1)} %copy-done.51, bf16[640,1024]{1,0:T(8,128)(2,1)} %collective-permute-done.16, bf16[320,1024]{1,0:T(8,128)(2,1)} %collective-permute-done.15, ...), kind=kOutput, calls=%fused_computation.8 | convolution fusion | flops 2742550528 | bytes 29097984 | tf_op jit(solution)/shard_map/dot_general | solution.py:145
  188.9 7.9 %fusion.92 = f32[640,2048]{1,0:T(8,128)} fusion(bf16[1024,640]{0,1:T(8,128)(2,1)} %copy-done.29, bf16[1024,2048]{1,0:T(8,128)(2,1)} %get-tuple-element.40), kind=kOutput, calls=%fused_computation.352 | convolution fusion | flops 2684354560 | bytes 10747904 | tf_op jit(solution)/shard_map/dot_general | solution.py:153
  196.8 4.5 fusion.91
  201.3 4.6 fusion.27
  206.0 5.1 multiply_reduce_fusion.3
  214.6 3.1 fusion.90
  217.7 3.2 convolution_convert_fusion.grad_ref
  221.0 15.5 %attend_back.1 = (f32[1024,1024]{1,0:T(8,128)S(1)}, f32[1536,256]{1,0:T(8,128)S(1)}, f32[1536,256]{1,0:T(8,128)S(1)}) custom-call(s32[1]{0:T(128)} %bitcast.4.first_ref, bf16[1024,1024]{1,0:T(8,128)(2,1)S(1)} %copy-done.1, bf16[1536,256]{1,0:T(8,128)(2,1)S(1)} %copy-done.3, bf16[1536,256]{1,0:T(8,128)(2,1)S(1)} %copy-done.5, ...), custom_call_target="tpu_custom_call" | custom-call | flops 8053063680 | bytes 13107200 | tf_op jit(solution)/shard_map/attend_back/pallas_call | solution.py:233
  239.4 5.4 %copy.64 = f32[1024,1024]{0,1:T(8,128)} copy(f32[1024,1024]{1,0:T(8,128)} %broadcast_multiply_fusion) | data formatting | bytes 8388608 | tf_op jit(solution)/shard_map/transpose(jvp())/mul | solution.py:308
  244.8 3.3 multiply_add_fusion.1
  256.1 3.1 slice.398
  272.6 3.1 slice.400
  282.2 7.9 %collective-permute-done.19 = bf16[1024,160]{0,1:T(8,128)(2,1)S(1)} collective-permute-done((bf16[1024,160]{0,1:T(8,128)(2,1)S(1)}, bf16[1024,160]{0,1:T(8,128)(2,1)S(1)}, u32[]{:S(2)}, u32[]{:S(2)}) %collective-permute-start.19) | collective-permute-done | bytes 327712 | tf_op jit(solution)/shard_map/ppermute | solution.py:66
  299.4 3.4 fusion.24
  315.3 21.9 %psum.7 = f32[1152]{0:T(1024)S(1)} all-reduce(f32[1152]{0:T(1024)S(1)} %pad_maximum_fusion.39), channel_id=1, replica_groups=mesh['dp'=8,'row'=2,'col'=2] {'dp'}, use_global_device_ids=true, to_apply=%region_18.19 | all-reduce | flops 1152 | bytes 9216 | tf_op jit(solution)/shard_map/psum | solution.py:402
  351.9 5.2 collective-permute-done.26
  359.2 4.5 dynamic_update_slice.32
  364.5 3.7 copy.78
  369.8 5.2 collective-permute-done.36
  377.2 5.4 %collective-permute-done.37 = bf16[320,128]{1,0:T(8,128)(2,1)S(1)} collective-permute-done((bf16[320,128]{1,0:T(8,128)(2,1)S(1)}, bf16[320,128]{1,0:T(8,128)(2,1)S(1)}, u32[]{:S(2)}, u32[]{:S(2)}) %collective-permute-start.37) | collective-permute-done | bytes 81952 | tf_op jit(solution)/shard_map/ppermute | solution.py:32
  382.8 3.9 collective-permute-done.38
  387.3 4.7 collective-permute-done.39
  392.7 4.2 collective-permute-done.40
  406.4 4.0 collective-permute-done.48
  411.3 4.0 collective-permute-done.31
  439.7 3.6 collective-permute-done.51
  445.0 3.6 collective-permute-done.34
  454.6 11.5 %collective-permute-done.53 = bf16[320,1024]{1,0:T(8,128)(2,1)S(1)} collective-permute-done((bf16[320,1024]{1,0:T(8,128)(2,1)S(1)}, bf16[320,1024]{1,0:T(8,128)(2,1)S(1)}, u32[]{:S(2)}, u32[]{:S(2)}) %collective-permute-start.53) | collective-permute-done | bytes 655392 | tf_op jit(solution)/shard_map/ppermute | solution.py:27
  470.9 4.8 collective-permute-done.54
  488.1 5.2 collective-permute-done.64
  493.3 3.4 collective-permute-done.56
  503.0 3.7 collective-permute-done.74
  513.0 4.5 collective-permute-done.75
  517.7 5.0 collective-permute-done.67
  (516 shorter events, 231.7 us)
Async XLA Ops:
  14.4 27.9 %collective-permute-start = (bf16[1024,160]{0,1:T(8,128)(2,1)}, bf16[1024,160]{0,1:T(8,128)(2,1)}, u32[]{:S(2)}, u32[]{:S(2)}) collective-permute-start(bf16[1024,160]{0,1:T(8,128)(2,1)} %bitcast.105), channel_id=1, source_target_pairs={{0,1},{1,0},{2,3},{3,2},{4,5},{5,4},{6,7},{7,6},{8,9},{9,8},{10,11... | collective-permute-start | bytes 983048 | tf_op jit(solution)/shard_map/ppermute | solution.py:45
  15.7 28.4 %collective-permute-start.1 = (bf16[1024,160]{0,1:T(8,128)(2,1)}, bf16[1024,160]{0,1:T(8,128)(2,1)}, u32[]{:S(2)}, u32[]{:S(2)}) collective-permute-start(bf16[1024,160]{0,1:T(8,128)(2,1)} %bitcast.104), channel_id=1, source_target_pairs={{0,2},{1,3},{2,0},{3,1},{4,6},{5,7},{6,4},{7,5},{8,10},{9,11},{10,... | collective-permute-start | bytes 983048 | tf_op jit(solution)/shard_map/ppermute | solution.py:45
  18.6 35.6 %collective-permute-start.7 = (bf16[320,512]{1,0:T(8,128)(2,1)}, bf16[320,512]{1,0:T(8,128)(2,1)}, u32[]{:S(2)}, u32[]{:S(2)}) collective-permute-start(bf16[320,512]{1,0:T(8,128)(2,1)} %param.17), channel_id=1, source_target_pairs={{0,2},{2,0},{1,3},{3,1},{4,6},{6,4},{5,7},{7,5},{8,10},{10,8},{9,1... | collective-permute-start | bytes 983048 | tf_op jit(solution)/shard_map/ppermute | solution.py:27
  18.9 76.2 %collective-permute-start.5 = (bf16[320,512]{1,0:T(8,128)(2,1)}, bf16[320,512]{1,0:T(8,128)(2,1)}, u32[]{:S(2)}, u32[]{:S(2)}) collective-permute-start(bf16[320,512]{1,0:T(8,128)(2,1)} %param.16), channel_id=1, source_target_pairs={{0,2},{2,0},{1,3},{3,1},{4,6},{6,4},{5,7},{7,5},{8,10},{10,8},{9,1... | collective-permute-start | bytes 983048 | tf_op jit(solution)/shard_map/ppermute | solution.py:27
  28.3 12.8 %collective-permute-start.4 = (f32[4,320]{1,0:T(4,128)S(1)}, f32[4,320]{1,0:T(4,128)S(1)}, u32[]{:S(2)}, u32[]{:S(2)}) collective-permute-start(f32[4,320]{1,0:T(4,128)S(1)} %pad_maximum_fusion.40), channel_id=1, source_target_pairs={{0,2},{2,0},{1,3},{3,1},{4,6},{6,4},{5,7},{7,5},{8,10},{10,8},{9,1... | collective-permute-start | bytes 15368 | tf_op jit(solution)/shard_map/ppermute | solution.py:27
  42.3 64.7 %collective-permute-start.11 = (bf16[320,1024]{1,0:T(8,128)(2,1)}, bf16[320,1024]{1,0:T(8,128)(2,1)}, u32[]{:S(2)}, u32[]{:S(2)}) collective-permute-start(bf16[320,1024]{1,0:T(8,128)(2,1)} %param.19), channel_id=1, source_target_pairs={{0,2},{2,0},{1,3},{3,1},{4,6},{6,4},{5,7},{7,5},{8,10},{10,8},{9,1... | collective-permute-start | bytes 1966088 | tf_op jit(solution)/shard_map/ppermute | solution.py:27
  44.2 65.2 %collective-permute-start.13 = (bf16[320,1024]{1,0:T(8,128)(2,1)}, bf16[320,1024]{1,0:T(8,128)(2,1)}, u32[]{:S(2)}, u32[]{:S(2)}) collective-permute-start(bf16[320,1024]{1,0:T(8,128)(2,1)} %param.20), channel_id=1, source_target_pairs={{0,2},{2,0},{1,3},{3,1},{4,6},{6,4},{5,7},{7,5},{8,10},{10,8},{9,1... | collective-permute-start | bytes 1966088 | tf_op jit(solution)/shard_map/ppermute | solution.py:27
  50.8 35.7 %collective-permute-start.21 = (bf16[1024,160]{0,1:T(8,128)(2,1)}, bf16[1024,160]{0,1:T(8,128)(2,1)S(1)}, u32[]{:S(2)}, u32[]{:S(2)}) collective-permute-start(bf16[1024,160]{0,1:T(8,128)(2,1)} %bitcast.101), channel_id=1, source_target_pairs={{0,2},{1,3},{2,0},{3,1},{4,6},{5,7},{6,4},{7,5},{8,10},{9,11},{10,... | collective-permute-start | bytes 983048 | tf_op jit(solution)/shard_map/ppermute | solution.py:45
  54.2 38.7 %collective-permute-start.22 = (bf16[1024,160]{0,1:T(8,128)(2,1)}, bf16[1024,160]{0,1:T(8,128)(2,1)S(1)}, u32[]{:S(2)}, u32[]{:S(2)}) collective-permute-start(bf16[1024,160]{0,1:T(8,128)(2,1)} %bitcast.100), channel_id=1, source_target_pairs={{0,3},{1,2},{2,1},{3,0},{4,7},{5,6},{6,5},{7,4},{8,11},{9,10},{10,... | collective-permute-start | bytes 983048 | tf_op jit(solution)/shard_map/ppermute | solution.py:45
  86.5 18.4 %collective-permute-start.9 = (bf16[320,512]{1,0:T(8,128)(2,1)}, bf16[320,512]{1,0:T(8,128)(2,1)}, u32[]{:S(2)}, u32[]{:S(2)}) collective-permute-start(bf16[320,512]{1,0:T(8,128)(2,1)} %bitcast.11), channel_id=1, source_target_pairs={{0,2},{2,0},{1,3},{3,1},{4,6},{6,4},{5,7},{7,5},{8,10},{10,8},{9,1... | collective-permute-start | bytes 983048 | tf_op jit(solution)/shard_map/ppermute | solution.py:27
  95.1 19.3 %collective-permute-start.15 = (bf16[320,1024]{1,0:T(8,128)(2,1)}, bf16[320,1024]{1,0:T(8,128)(2,1)}, u32[]{:S(2)}, u32[]{:S(2)}) collective-permute-start(bf16[320,1024]{1,0:T(8,128)(2,1)} %bitcast.12), channel_id=1, source_target_pairs={{0,2},{2,0},{1,3},{3,1},{4,6},{6,4},{5,7},{7,5},{8,10},{10,8},{9,1... | collective-permute-start | bytes 1966088 | tf_op jit(solution)/shard_map/ppermute | solution.py:27
  100.5 16.4 %collective-permute-start.8 = (bf16[512,512]{1,0:T(8,128)(2,1)}, bf16[512,512]{1,0:T(8,128)(2,1)S(1)}, u32[]{:S(2)}, u32[]{:S(2)}) collective-permute-start(bf16[512,512]{1,0:T(8,128)(2,1)} %fusion.53), channel_id=1, source_target_pairs={{0,1},{1,2},{2,3},{4,5},{5,6},{6,7},{8,9},{9,10},{10,11},{12,13},{... | collective-permute-start | bytes 1572872 | tf_op jit(solution)/shard_map/ppermute | solution.py:315
  104.9 15.7 %collective-permute-start.6 = (bf16[640,512]{1,0:T(8,128)(2,1)}, bf16[640,512]{1,0:T(8,128)(2,1)S(1)}, u32[]{:S(2)}, u32[]{:S(2)}) collective-permute-start(bf16[640,512]{1,0:T(8,128)(2,1)} %copy-done.60), channel_id=1, source_target_pairs={{0,1},{1,0},{2,3},{3,2},{4,5},{5,4},{6,7},{7,6},{8,9},{9,8},{10,11... | collective-permute-start | bytes 1966088 | tf_op jit(solution)/shard_map/ppermute | solution.py:27
  107.1 33.2 %collective-permute-start.10 = (bf16[640,512]{1,0:T(8,128)(2,1)}, bf16[640,512]{1,0:T(8,128)(2,1)}, u32[]{:S(2)}, u32[]{:S(2)}) collective-permute-start(bf16[640,512]{1,0:T(8,128)(2,1)} %pad_maximum_fusion.19), channel_id=1, source_target_pairs={{0,1},{1,0},{2,3},{3,2},{4,5},{5,4},{6,7},{7,6},{8,9},{9,8},{10,11... | collective-permute-start | bytes 1966088 | tf_op jit(solution)/shard_map/ppermute | solution.py:27
  109.3 34.8 %collective-permute-start.12 = (bf16[640,1024]{1,0:T(8,128)(2,1)}, bf16[640,1024]{1,0:T(8,128)(2,1)}, u32[]{:S(2)}, u32[]{:S(2)}) collective-permute-start(bf16[640,1024]{1,0:T(8,128)(2,1)} %constant_dynamic-update-slice_fusion.4), channel_id=1, source_target_pairs={{0,1},{1,0},{2,3},{3,2},{4,5},{5,4},{6,7},{7,6},{8,9},{9,8},{10,11... | collective-permute-start | bytes 3932168 | tf_op jit(solution)/shard_map/ppermute | solution.py:27
  114.4 35.5 %collective-permute-start.14 = (bf16[640,1024]{1,0:T(8,128)(2,1)}, bf16[640,1024]{1,0:T(8,128)(2,1)}, u32[]{:S(2)}, u32[]{:S(2)}) collective-permute-start(bf16[640,1024]{1,0:T(8,128)(2,1)} %constant_dynamic-update-slice_fusion.6), channel_id=1, source_target_pairs={{0,1},{1,0},{2,3},{3,2},{4,5},{5,4},{6,7},{7,6},{8,9},{9,8},{10,11... | collective-permute-start | bytes 3932168 | tf_op jit(solution)/shard_map/ppermute | solution.py:27
  116.8 42.5 %collective-permute-start.16 = (bf16[640,1024]{1,0:T(8,128)(2,1)}, bf16[640,1024]{1,0:T(8,128)(2,1)}, u32[]{:S(2)}, u32[]{:S(2)}) collective-permute-start(bf16[640,1024]{1,0:T(8,128)(2,1)} %pad_maximum_fusion.12), channel_id=1, source_target_pairs={{0,1},{1,0},{2,3},{3,2},{4,5},{5,4},{6,7},{7,6},{8,9},{9,8},{10,11... | collective-permute-start | bytes 3932168 | tf_op jit(solution)/shard_map/ppermute | solution.py:27
  254.5 36.8 %collective-permute-start.23 = (bf16[512,512]{1,0:T(8,128)(2,1)}, bf16[512,512]{1,0:T(8,128)(2,1)}, u32[]{:S(2)}, u32[]{:S(2)}) collective-permute-start(bf16[512,512]{1,0:T(8,128)(2,1)} %pad_maximum_fusion.25), channel_id=1, source_target_pairs={{1,0},{2,1},{3,2},{5,4},{6,5},{7,6},{9,8},{10,9},{11,10},{13,12},{... | collective-permute-start | bytes 1572872 | tf_op jit(solution)/shard_map/ppermute | solution.py:358
  259.2 159.2 %collective-permute-start.68 = (bf16[640,1024]{1,0:T(8,128)(2,1)}, bf16[640,1024]{1,0:T(8,128)(2,1)}, u32[]{:S(2)}, u32[]{:S(2)}) collective-permute-start(bf16[640,1024]{1,0:T(8,128)(2,1)} %slice.398), channel_id=1, source_target_pairs={{0,1},{1,0},{2,3},{3,2},{4,5},{5,4},{6,7},{7,6},{8,9},{9,8},{10,11... | collective-permute-start | bytes 3932168 | tf_op jit(solution)/shard_map/ppermute | solution.py:27
  263.4 157.3 %collective-permute-start.60 = (bf16[640,1024]{1,0:T(8,128)(2,1)}, bf16[640,1024]{1,0:T(8,128)(2,1)}, u32[]{:S(2)}, u32[]{:S(2)}) collective-permute-start(bf16[640,1024]{1,0:T(8,128)(2,1)} %slice.399), channel_id=1, source_target_pairs={{0,1},{1,0},{2,3},{3,2},{4,5},{5,4},{6,7},{7,6},{8,9},{9,8},{10,11... | collective-permute-start | bytes 3932168 | tf_op jit(solution)/shard_map/ppermute | solution.py:27
  264.6 15.6 %collective-permute-start.17 = (bf16[1024,160]{0,1:T(8,128)(2,1)}, bf16[1024,160]{0,1:T(8,128)(2,1)}, u32[]{:S(2)}, u32[]{:S(2)}) collective-permute-start(bf16[1024,160]{0,1:T(8,128)(2,1)} %get-tuple-element.57), channel_id=1, source_target_pairs={{0,1},{1,0},{2,3},{3,2},{4,5},{5,4},{6,7},{7,6},{8,9},{9,8},{10,11... | collective-permute-start | bytes 983048 | tf_op jit(solution)/shard_map/ppermute | solution.py:66
  268.0 13.2 %collective-permute-start.18 = (bf16[1024,160]{0,1:T(8,128)(2,1)}, bf16[1024,160]{0,1:T(8,128)(2,1)}, u32[]{:S(2)}, u32[]{:S(2)}) collective-permute-start(bf16[1024,160]{0,1:T(8,128)(2,1)} %get-tuple-element.58), channel_id=1, source_target_pairs={{0,2},{1,3},{2,0},{3,1},{4,6},{5,7},{6,4},{7,5},{8,10},{9,11},{10,... | collective-permute-start | bytes 983048 | tf_op jit(solution)/shard_map/ppermute | solution.py:66
  280.2 10.0 %collective-permute-start.19 = (bf16[1024,160]{0,1:T(8,128)(2,1)S(1)}, bf16[1024,160]{0,1:T(8,128)(2,1)S(1)}, u32[]{:S(2)}, u32[]{:S(2)}) collective-permute-start(bf16[1024,160]{0,1:T(8,128)(2,1)S(1)} %copy-done.56), channel_id=1, source_target_pairs={{0,3},{1,2},{2,1},{3,0},{4,7},{5,6},{6,5},{7,4},{8,11},{9,10},{10,... | collective-permute-start | bytes 983048 | tf_op jit(solution)/shard_map/ppermute | solution.py:66
  310.4 28.1 %collective-permute-start.44 = (bf16[640,512]{1,0:T(8,128)(2,1)}, bf16[640,512]{1,0:T(8,128)(2,1)}, u32[]{:S(2)}, u32[]{:S(2)}) collective-permute-start(bf16[640,512]{1,0:T(8,128)(2,1)} %slice.404), channel_id=1, source_target_pairs={{0,1},{1,0},{2,3},{3,2},{4,5},{5,4},{6,7},{7,6},{8,9},{9,8},{10,11... | collective-permute-start | bytes 1966088 | tf_op jit(solution)/shard_map/ppermute | solution.py:27
  310.5 29.7 %collective-permute-start.27 = (bf16[640,512]{1,0:T(8,128)(2,1)S(1)}, bf16[640,512]{1,0:T(8,128)(2,1)}, u32[]{:S(2)}, u32[]{:S(2)}) collective-permute-start(bf16[640,512]{1,0:T(8,128)(2,1)S(1)} %copy-done.53), channel_id=1, source_target_pairs={{0,1},{1,0},{2,3},{3,2},{4,5},{5,4},{6,7},{7,6},{8,9},{9,8},{10,11... | collective-permute-start | bytes 1966088 | tf_op jit(solution)/shard_map/ppermute | solution.py:27
  315.3 29.6 %collective-permute-start.35 = (bf16[640,256]{1,0:T(8,128)(2,1)}, bf16[640,256]{1,0:T(8,128)(2,1)}, u32[]{:S(2)}, u32[]{:S(2)}) collective-permute-start(bf16[640,256]{1,0:T(8,128)(2,1)} %dynamic-slice_convert_fusion.3), channel_id=1, source_target_pairs={{0,1},{1,0},{2,3},{3,2},{4,5},{5,4},{6,7},{7,6},{8,9},{9,8},{10,11... | collective-permute-start | bytes 983048 | tf_op jit(solution)/shard_map/ppermute | solution.py:27
  340.2 10.6 %collective-permute-start.25 = (bf16[1024,160]{0,1:T(8,128)(2,1)S(1)}, bf16[1024,160]{0,1:T(8,128)(2,1)S(1)}, u32[]{:S(2)}, u32[]{:S(2)}) collective-permute-start(bf16[1024,160]{0,1:T(8,128)(2,1)S(1)} %copy-done.55), channel_id=1, source_target_pairs={{0,2},{1,3},{2,0},{3,1},{4,6},{5,7},{6,4},{7,5},{8,10},{9,11},{10,... | collective-permute-start | bytes 983048 | tf_op jit(solution)/shard_map/ppermute | solution.py:66
  344.9 12.1 %collective-permute-start.26 = (bf16[1024,160]{0,1:T(8,128)(2,1)S(1)}, bf16[1024,160]{0,1:T(8,128)(2,1)S(1)}, u32[]{:S(2)}, u32[]{:S(2)}) collective-permute-start(bf16[1024,160]{0,1:T(8,128)(2,1)S(1)} %copy-done.54), channel_id=1, source_target_pairs={{0,3},{1,2},{2,1},{3,0},{4,7},{5,6},{6,5},{7,4},{8,11},{9,10},{10,... | collective-permute-start | bytes 983048 | tf_op jit(solution)/shard_map/ppermute | solution.py:66
  346.6 21.6 %collective-permute-start.45 = (bf16[320,512]{1,0:T(8,128)(2,1)}, bf16[320,512]{1,0:T(8,128)(2,1)}, u32[]{:S(2)}, u32[]{:S(2)}) collective-permute-start(bf16[320,512]{1,0:T(8,128)(2,1)} %slice.406), channel_id=1, source_target_pairs={{0,2},{2,0},{1,3},{3,1},{4,6},{6,4},{5,7},{7,5},{8,10},{10,8},{9,1... | collective-permute-start | bytes 983048 | tf_op jit(solution)/shard_map/ppermute | solution.py:27
  350.8 73.6 %collective-permute-start.52 = (bf16[640,1024]{1,0:T(8,128)(2,1)}, bf16[640,1024]{1,0:T(8,128)(2,1)}, u32[]{:S(2)}, u32[]{:S(2)}) collective-permute-start(bf16[640,1024]{1,0:T(8,128)(2,1)} %slice.400), channel_id=1, source_target_pairs={{0,1},{1,0},{2,3},{3,2},{4,5},{5,4},{6,7},{7,6},{8,9},{9,8},{10,11... | collective-permute-start | bytes 3932168 | tf_op jit(solution)/shard_map/ppermute | solution.py:27
  357.0 18.0 %collective-permute-start.28 = (bf16[320,512]{1,0:T(8,128)(2,1)}, bf16[320,512]{1,0:T(8,128)(2,1)S(1)}, u32[]{:S(2)}, u32[]{:S(2)}) collective-permute-start(bf16[320,512]{1,0:T(8,128)(2,1)} %slice.407), channel_id=1, source_target_pairs={{0,2},{2,0},{1,3},{3,1},{4,6},{6,4},{5,7},{7,5},{8,10},{10,8},{9,1... | collective-permute-start | bytes 983048 | tf_op jit(solution)/shard_map/ppermute | solution.py:27
  375.0 12.1 %collective-permute-start.46 = (bf16[320,256]{1,0:T(8,128)(2,1)S(1)}, bf16[320,256]{1,0:T(8,128)(2,1)S(1)}, u32[]{:S(2)}, u32[]{:S(2)}) collective-permute-start(bf16[320,256]{1,0:T(8,128)(2,1)S(1)} %dynamic-slice_convert_fusion.7), channel_id=1, source_target_pairs={{0,4},{4,0},{8,12},{12,8},{16,20},{20,16},{24,28},{28,24},{1,5},{5... | collective-permute-start | bytes 491528 | tf_op jit(solution)/shard_map/ppermute | solution.py:32
  392.0 11.0 %collective-permute-start.47 = (bf16[320,128]{1,0:T(8,128)(2,1)S(1)}, bf16[320,128]{1,0:T(8,128)(2,1)S(1)}, u32[]{:S(2)}, u32[]{:S(2)}) collective-permute-start(bf16[320,128]{1,0:T(8,128)(2,1)S(1)} %dynamic-slice_convert_fusion.12), channel_id=1, source_target_pairs={{0,8},{4,12},{8,0},{12,4},{16,24},{20,28},{24,16},{28,20},{1,9},{5... | collective-permute-start | bytes 245768 | tf_op jit(solution)/shard_map/ppermute | solution.py:32
  403.0 13.2 %collective-permute-start.42 = (bf16[320,128]{1,0:T(8,128)(2,1)S(1)}, bf16[320,128]{1,0:T(8,128)(2,1)S(1)}, u32[]{:S(2)}, u32[]{:S(2)}) collective-permute-start(bf16[320,128]{1,0:T(8,128)(2,1)S(1)} %pad_maximum_fusion.35), channel_id=1, source_target_pairs={{0,4},{4,0},{8,12},{12,8},{16,20},{20,16},{24,28},{28,24},{1,5},{5... | collective-permute-start | bytes 245768 | tf_op jit(solution)/shard_map/ppermute | solution.py:32
  415.3 11.7 %collective-permute-start.49 = (bf16[160,128]{1,0:T(8,128)(2,1)S(1)}, bf16[160,128]{1,0:T(8,128)(2,1)S(1)}, u32[]{:S(2)}, u32[]{:S(2)}) collective-permute-start(bf16[160,128]{1,0:T(8,128)(2,1)S(1)} %add_convert_fusion.4), channel_id=1, source_target_pairs={{0,16},{4,20},{8,24},{12,28},{16,0},{20,4},{24,8},{28,12},{1,17},{... | collective-permute-start | bytes 122888 | tf_op jit(solution)/shard_map/ppermute | solution.py:32
  416.2 12.5 %collective-permute-start.32 = (bf16[160,128]{1,0:T(8,128)(2,1)S(1)}, bf16[160,128]{1,0:T(8,128)(2,1)S(1)}, u32[]{:S(2)}, u32[]{:S(2)}) collective-permute-start(bf16[160,128]{1,0:T(8,128)(2,1)S(1)} %add_convert_fusion.5), channel_id=1, source_target_pairs={{0,16},{4,20},{8,24},{12,28},{16,0},{20,4},{24,8},{28,12},{1,17},{... | collective-permute-start | bytes 122888 | tf_op jit(solution)/shard_map/ppermute | solution.py:32
  418.4 32.1 %collective-permute-start.43 = (f32[320,256]{1,0:T(8,128)S(1)}, f32[320,256]{1,0:T(8,128)S(1)}, u32[]{:S(2)}, u32[]{:S(2)}) collective-permute-start(f32[320,256]{1,0:T(8,128)S(1)} %maximum_convert_fusion.3), channel_id=1, source_target_pairs={{0,1},{1,0},{2,3},{3,2},{4,5},{5,4},{6,7},{7,6},{8,9},{9,8},{10,11... | collective-permute-start | bytes 983048 | tf_op jit(solution)/shard_map/ppermute | solution.py:27
  420.8 30.8 %collective-permute-start.69 = (bf16[320,1024]{1,0:T(8,128)(2,1)S(1)}, bf16[320,1024]{1,0:T(8,128)(2,1)S(1)}, u32[]{:S(2)}, u32[]{:S(2)}) collective-permute-start(bf16[320,1024]{1,0:T(8,128)(2,1)S(1)} %slice.401), channel_id=1, source_target_pairs={{0,2},{2,0},{1,3},{3,1},{4,6},{6,4},{5,7},{7,5},{8,10},{10,8},{9,1... | collective-permute-start | bytes 1966088 | tf_op jit(solution)/shard_map/ppermute | solution.py:27
  424.4 29.0 %collective-permute-start.61 = (bf16[320,1024]{1,0:T(8,128)(2,1)S(1)}, bf16[320,1024]{1,0:T(8,128)(2,1)S(1)}, u32[]{:S(2)}, u32[]{:S(2)}) collective-permute-start(bf16[320,1024]{1,0:T(8,128)(2,1)S(1)} %slice.402), channel_id=1, source_target_pairs={{0,2},{2,0},{1,3},{3,1},{4,6},{6,4},{5,7},{7,5},{8,10},{10,8},{9,1... | collective-permute-start | bytes 1966088 | tf_op jit(solution)/shard_map/ppermute | solution.py:27
  427.0 39.0 %collective-permute-start.53 = (bf16[320,1024]{1,0:T(8,128)(2,1)S(1)}, bf16[320,1024]{1,0:T(8,128)(2,1)S(1)}, u32[]{:S(2)}, u32[]{:S(2)}) collective-permute-start(bf16[320,1024]{1,0:T(8,128)(2,1)S(1)} %slice.403), channel_id=1, source_target_pairs={{0,2},{2,0},{1,3},{3,1},{4,6},{6,4},{5,7},{7,5},{8,10},{10,8},{9,1... | collective-permute-start | bytes 1966088 | tf_op jit(solution)/shard_map/ppermute | solution.py:27
  451.8 16.4 %collective-permute-start.70 = (bf16[320,512]{1,0:T(8,128)(2,1)S(1)}, bf16[320,512]{1,0:T(8,128)(2,1)S(1)}, u32[]{:S(2)}, u32[]{:S(2)}) collective-permute-start(bf16[320,512]{1,0:T(8,128)(2,1)S(1)} %dynamic-slice_convert_fusion), channel_id=1, source_target_pairs={{0,4},{4,0},{8,12},{12,8},{16,20},{20,16},{24,28},{28,24},{1,5},{5... | collective-permute-start | bytes 983048 | tf_op jit(solution)/shard_map/ppermute | solution.py:32
  453.7 17.0 %collective-permute-start.62 = (bf16[320,512]{1,0:T(8,128)(2,1)S(1)}, bf16[320,512]{1,0:T(8,128)(2,1)S(1)}, u32[]{:S(2)}, u32[]{:S(2)}) collective-permute-start(bf16[320,512]{1,0:T(8,128)(2,1)S(1)} %dynamic-slice_convert_fusion.1), channel_id=1, source_target_pairs={{0,4},{4,0},{8,12},{12,8},{16,20},{20,16},{24,28},{28,24},{1,5},{5... | collective-permute-start | bytes 983048 | tf_op jit(solution)/shard_map/ppermute | solution.py:32
  479.8 13.4 %collective-permute-start.64 = (bf16[320,128]{1,0:T(8,128)(2,1)S(1)}, bf16[320,128]{1,0:T(8,128)(2,1)S(1)}, u32[]{:S(2)}, u32[]{:S(2)}) collective-permute-start(bf16[320,128]{1,0:T(8,128)(2,1)S(1)} %dynamic-slice_convert_fusion.10), channel_id=1, source_target_pairs={{0,16},{4,20},{8,24},{12,28},{16,0},{20,4},{24,8},{28,12},{1,17},{... | collective-permute-start | bytes 245768 | tf_op jit(solution)/shard_map/ppermute | solution.py:32
  483.0 13.7 %collective-permute-start.56 = (bf16[320,128]{1,0:T(8,128)(2,1)S(1)}, bf16[320,128]{1,0:T(8,128)(2,1)S(1)}, u32[]{:S(2)}, u32[]{:S(2)}) collective-permute-start(bf16[320,128]{1,0:T(8,128)(2,1)S(1)} %dynamic-slice_convert_fusion.11), channel_id=1, source_target_pairs={{0,16},{4,20},{8,24},{12,28},{16,0},{20,4},{24,8},{28,12},{1,17},{... | collective-permute-start | bytes 245768 | tf_op jit(solution)/shard_map/ppermute | solution.py:32
  488.0 11.5 %collective-permute-start.73 = (bf16[320,128]{1,0:T(8,128)(2,1)S(1)}, bf16[320,128]{1,0:T(8,128)(2,1)S(1)}, u32[]{:S(2)}, u32[]{:S(2)}) collective-permute-start(bf16[320,128]{1,0:T(8,128)(2,1)S(1)} %add_convert_fusion.1), channel_id=1, source_target_pairs={{0,16},{4,20},{8,24},{12,28},{16,0},{20,4},{24,8},{28,12},{1,17},{... | collective-permute-start | bytes 245768 | tf_op jit(solution)/shard_map/ppermute | solution.py:32
  506.8 10.7 %collective-permute-start.75 = (bf16[320,512]{1,0:T(8,128)(2,1)S(1)}, bf16[320,512]{1,0:T(8,128)(2,1)S(1)}, u32[]{:S(2)}, u32[]{:S(2)}) collective-permute-start(bf16[320,512]{1,0:T(8,128)(2,1)S(1)} %pad_maximum_fusion.28), channel_id=1, source_target_pairs={{0,4},{4,0},{8,12},{12,8},{16,20},{20,16},{24,28},{28,24},{1,5},{5... | collective-permute-start | bytes 983048 | tf_op jit(solution)/shard_map/ppermute | solution.py:32
  509.5 13.1 %collective-permute-start.67 = (bf16[320,512]{1,0:T(8,128)(2,1)S(1)}, bf16[320,512]{1,0:T(8,128)(2,1)S(1)}, u32[]{:S(2)}, u32[]{:S(2)}) collective-permute-start(bf16[320,512]{1,0:T(8,128)(2,1)S(1)} %pad_maximum_fusion.27), channel_id=1, source_target_pairs={{0,4},{4,0},{8,12},{12,8},{16,20},{20,16},{24,28},{28,24},{1,5},{5... | collective-permute-start | bytes 983048 | tf_op jit(solution)/shard_map/ppermute | solution.py:32
  511.4 14.8 %collective-permute-start.59 = (bf16[320,512]{1,0:T(8,128)(2,1)S(1)}, bf16[320,512]{1,0:T(8,128)(2,1)S(1)}, u32[]{:S(2)}, u32[]{:S(2)}) collective-permute-start(bf16[320,512]{1,0:T(8,128)(2,1)S(1)} %pad_maximum_fusion.26), channel_id=1, source_target_pairs={{0,4},{4,0},{8,12},{12,8},{16,20},{20,16},{24,28},{28,24},{1,5},{5... | collective-permute-start | bytes 983048 | tf_op jit(solution)/shard_map/ppermute | solution.py:32
  (113 other events, 1120.8 us)
